TPU v7x, 128 devices: a whole 4x4x4 slice. The times are simulated.
128 devices in a mesh: vrow: 8 (over y_lo, z), aux: 8 (over x, core), pair: 2 (over y_hi).
Axes of the slice: x: 4, y: 4 (y_hi: 2, y_lo: 2; y = y_hi * 2 + y_lo), z: 4, core: 2. Of those that a mesh axis runs over, the one named last changes fastest.
Arguments:
- factors: bfloat16 [64, 1920, 960], P(('vrow', 'pair'), 'aux'), may hold values from -6 to 6
- amplitudes: bfloat16 [4, 960, 960], replicated, may hold values from -0.00015258789 to 0.00015258789
Outputs:
- ladder: float32 [4, 64, 64], P(None, ('vrow', 'pair'))
All inputs are finite; a program needn't handle non-finite values.
Results may differ from a plain program's by a relative error of at most 0.0029.
Values may be sent and summed in bfloat16 or wider, within the bound.
No kernel may reach another device: no remote copies, remote signals or barrier semaphores. Data moves between devices by JAX's collectives and lax.ppermute only.
A program may use at most 192 MiB of HBM per device.

v0:
```python
import jax
import jax.numpy as jnp
from jax import lax
from jax.sharding import PartitionSpec as P


def half_terms(blocks, amplitudes):
    nrows, nq, width = blocks.shape
    flat = blocks.reshape(nrows * nq, width)
    mixed = jnp.einsum("kc,pcd->kpd", flat, amplitudes, preferred_element_type=jnp.float32)
    return mixed.astype(jnp.bfloat16).reshape(nrows, nq, amplitudes.shape[0], width)


def local(factors, amplitudes):
    halves = half_terms(factors, amplitudes)
    partial_sum = jnp.einsum(
        "nuio,tuo->nit",
        halves,
        lax.all_gather(factors, ("vrow", "pair"), axis=0, tiled=True),
        preferred_element_type=jnp.float32,
    )
    summed = lax.psum(partial_sum, "aux")
    return jnp.transpose(summed, (1, 0, 2))


def solution(mesh):
    in_specs = (P(("vrow", "pair"), "aux", None), P())
    out_specs = P(None, ("vrow", "pair"), None)
    return jax.shard_map(local, mesh=mesh, in_specs=in_specs, out_specs=out_specs, check_vma=False)
```

profile of v0, /device:TPU:0, one launch (start us, length us, event | category | flops | bytes accessed | tf_op | source)
XLA Modules:
  0.0 754.6 jit_solution(5586202503463857373)
XLA Ops:
  6.5 0.0 all-gather.2.cloned.1.call-start
  6.5 0.7 all-gather.2.cloned.1.call-update
  7.3 13.2 %convolution_convert_fusion = bf16[960,4,960]{2,0,1:T(8,128)(2,1)} fusion(bf16[960,960,1]{1,0,2:T(8,128)(2,1)} %bitcast.18, bf16[4,960,960]{2,1,0:T(8,128)(2,1)} %param.3), kind=kOutput, calls=%fused_computation.2 | convolution fusion | flops 7081574400 | bytes 16588800 | tf_op jit(solution)/shard_map/kc,pcd->kpd/dot_general | solution.py:10
  20.5 13.7 %copy.6 = bf16[4,240,4,960]{1,2,3,0:T(4,128)(2,1)} copy(bf16[4,240,4,960]{3,1,0,2:T(8,128)(2,1)} %bitcast.17) | data formatting | bytes 14745600 | tf_op jit(solution)/shard_map/reshape | solution.py:11
  34.2 637.9 %all-gather.2.cloned.1.call-done = bf16[64,240,960]{2,1,0:T(8,128)(2,1)} async-done(((bf16[4,240,960]{2,1,0:T(8,128)(2,1)}), bf16[64,240,960]{2,1,0:T(8,128)(2,1)}) %all-gather.2.cloned.1.call-update) | async-done | bytes 29491216 | tf_op jit(solution)/shard_map/all_gather | solution.py:19
  672.1 44.7 %copy.7 = bf16[64,240,960]{1,0,2:T(8,128)(2,1)} copy(bf16[64,240,960]{2,1,0:T(8,128)(2,1)} %all-gather.2.cloned.1.call-done) | data formatting | bytes 58982400 | tf_op jit(solution)/shard_map/all_gather | solution.py:19
  716.7 16.6 %fusion.2 = f32[4,4,64]{2,0,1:T(4,128)S(1)} fusion(bf16[4,240,4,960]{1,2,3,0:T(4,128)(2,1)} %copy.6, bf16[64,240,960]{1,0,2:T(8,128)(2,1)} %copy.7), kind=kOutput, calls=%fused_computation.3 | convolution fusion | flops 471859200 | bytes 36868096 | tf_op jit(solution)/shard_map/nuio,tuo->nit/dot_general | solution.py:16
  733.4 13.8 %psum.7 = f32[4,4,64]{2,0,1:T(4,128)S(1)} all-reduce(f32[4,4,64]{2,0,1:T(4,128)S(1)} %fusion.2), channel_id=1, replica_groups=mesh['vrow'=8,'aux'=8,'pair'=2] {'aux'}, use_global_device_ids=true, to_apply=%region_0.0 | all-reduce | flops 1024 | bytes 8192 | tf_op jit(solution)/shard_map/psum | solution.py:22
  747.2 0.6 copy.8
Async XLA Ops:
  6.5 665.5 %all-gather.2.cloned.1.call-start = ((), (), s32[]{:S(2)}) async-start(), calls=%async_computation | async-start | bytes 33423360 | tf_op jit(solution)/shard_map/all_gather | solution.py:19
Sparse Core Ops, SparseCore 0:
  9.0 663.0 all-gather.1
where the time goes:
time: 756 us; the launch traced here: 755 us
  waiting for transfers between devices  639 us (85%)
  local copies, waits for them, and re-layouts  58.9 us (8%)
  matrix products  29.9 us (4%)
  blocking collectives  13.8 us (2%)
  between operations  13.4 us (2%)
    all_gather x1, waiting for transfers between devices, local(): lax.all_gather(factors, ('vrow', 'pair'), axis=0, tiled=True)  638 us
    all_gather x1, local copies, waits for them, and re-layouts, local(): lax.all_gather(factors, ('vrow', 'pair'), axis=0, tiled=True)  44.7 us
    dot_general x1, matrix products, local(): jnp.einsum('nuio,tuo->nit', halves, lax.all_gather(factors, ('vrow', 'pai...  16.6 us
  transfers between devices with their start and end apart: 1, of which 1 were waited for; matrix products, arithmetic and copies ran while one was open for 4% of the time, Pallas kernels for 0%

commit v1 on v0

v1 whole, which is shorter than its diff:
```python
import jax
import jax.numpy as jnp
from jax import lax
from jax.sharding import PartitionSpec as P

ROWS = ("vrow", "pair")


def local(factors, amplitudes):
    mine = lax.all_to_all(factors, ROWS, split_axis=1, concat_axis=0, tiled=True)
    half = jnp.einsum("aqc,pcd->paqd", mine, amplitudes, preferred_element_type=jnp.float32)
    half = half.astype(jnp.bfloat16)
    terms = jnp.einsum("paqd,bqd->pab", half, mine, preferred_element_type=jnp.float32)
    terms = lax.psum_scatter(terms, ROWS, scatter_dimension=1, tiled=True)
    return lax.psum(terms, "aux")


def solution(mesh):
    in_specs = (P(ROWS, "aux", None), P())
    out_specs = P(None, ROWS, None)
    return jax.shard_map(local, mesh=mesh, in_specs=in_specs, out_specs=out_specs, check_vma=False)
```

time: 756 us -> 169 us (0.22)
  waiting for transfers between devices: 639 us -> 79.3 us
  local copies, waits for them, and re-layouts: 58.9 us -> 7.62 us
  blocking collectives: 13.8 us -> 48.4 us
  matrix products: 29.9 us -> 19.3 us
    all_gather x1 -> x0, waiting for transfers between devices: 638 us -> none  [local(): lax.all_gather(factors, ('vrow', 'pair'), axis=0, tiled=True)]
    unnamed x1 -> x2, waiting for transfers between devices: 0.71 us -> 79.3 us
    all_gather x1 -> x0, local copies, waits for them, and re-layouts: 44.7 us -> none  [local(): lax.all_gather(factors, ('vrow', 'pair'), axis=0, tiled=True)]
    all_to_all x0 -> x1, blocking collectives: none -> 34.6 us  [local(): lax.all_to_all(factors, ROWS, split_axis=1, concat_axis=0, tiled=True)]
    reshape x1 -> x0, local copies, waits for them, and re-layouts: 13.7 us -> none  [half_terms(): mixed.astype(jnp.bfloat16).reshape(nrows, nq, amplitudes.shape[0], width)]
    dot_general x2 -> x1, matrix products: 29.9 us -> 19.3 us  [local(): jnp.einsum('paqd,bqd->pab', half, mine, preferred_element_type=jnp.float32)]
  transfers between devices with their start and end apart: 1 -> 1, of which waited for: 1 -> 1; matrix products, arithmetic and copies ran while one was open for 4% -> 0% of each run, Pallas kernels for 0% -> 0%
where the time goes in v1:
time: 169 us
  waiting for transfers between devices  79.3 us (47%)
  blocking collectives  48.4 us (29%)
  matrix products  19.3 us (11%)
  between operations  14.1 us (8%)
  local copies, waits for them, and re-layouts  7.62 us (5%)
    unnamed x2, waiting for transfers between devices  79.3 us
    all_to_all x1, blocking collectives, local(): lax.all_to_all(factors, ROWS, split_axis=1, concat_axis=0, tiled=True)  34.6 us
    dot_general x1, matrix products, local(): jnp.einsum('paqd,bqd->pab', half, mine, preferred_element_type=jnp.float32)  19.3 us
    psum x1, blocking collectives, local(): return lax.psum(terms, 'aux')  13.8 us
    unnamed x5, local copies, waits for them, and re-layouts  4.37 us
  transfers between devices with their start and end apart: 1, of which 1 were waited for; matrix products, arithmetic and copies ran while one was open for 0% of the time, Pallas kernels for 0%

profile of v1, /device:TPU:0, one launch (start us, length us, event | category | flops | bytes accessed | tf_op | source)
XLA Modules:
  0.0 168.7 jit_solution(15607283902779358041)
XLA Ops:
  6.5 0.0 all-reduce.3.cloned.1.call-start
  6.5 3.1 %copy.6 = bf16[4,240,960]{2,0,1:T(4,128)(2,1)S(1)} copy(bf16[4,240,960]{2,1,0:T(8,128)(2,1)} %param.2) | data formatting | bytes 3686400 | tf_op args[0]
  9.6 34.6 %all_to_all.18 = bf16[4,240,960]{2,0,1:T(4,128)(2,1)S(1)} all-to-all(bf16[4,240,960]{2,0,1:T(4,128)(2,1)S(1)} %copy.6), channel_id=1, replica_groups=mesh['vrow'=8,'aux'=8,'pair'=2] {'vrow','pair'}, dimensions={1} | all-to-all | bytes 3686400 | tf_op jit(solution)/shard_map/all_to_all | solution.py:10
  44.2 0.9 copy.7
  45.2 2.3 %reshape.1 = bf16[64,15,960,1]{2,0,1,3:T(8,128)(2,1)} reshape(bf16[16,4,15,960]{3,1,0,2:T(4,128)(2,1)S(1)} %copy.7) | data formatting | bytes 3686400 | tf_op jit(solution)/shard_map/all_to_all | solution.py:10
  47.5 0.0 copy-start
  47.5 19.3 %fusion.9 = f32[4,64,64]{2,1,0:T(8,128)} fusion(bf16[64,15,960,1]{2,0,1,3:T(8,128)(2,1)} %reshape.1, bf16[4,960,960]{2,1,0:T(8,128)(2,1)} %param.3), kind=kOutput, calls=%fused_computation.5 | convolution fusion | flops 7553433600 | bytes 9281536 | tf_op jit(solution)/shard_map/paqd,bqd->pab/dot_general | solution.py:13
  66.8 0.0 all-reduce.3.cloned.1.call-update
  66.8 0.0 copy-done
  66.8 0.6 dynamic-slice
  68.1 79.3 %all-reduce.3.cloned.1.call-done = f32[4,64,64]{2,1,0:T(8,128)} async-done(((f32[4,64,64]{2,1,0:T(8,128)}), f32[4,64,64]{2,1,0:T(8,128)}) %all-reduce.3.cloned.1.call-update) | async-done | bytes 65552
  147.3 0.7 constant_dynamic-slice_fusion
  148.1 13.8 %psum.7 = f32[4,4,64]{2,1,0:T(4,128)} all-reduce(f32[4,4,64]{2,1,0:T(4,128)S(1)} %constant_dynamic-slice_fusion), channel_id=1, replica_groups=mesh['vrow'=8,'aux'=8,'pair'=2] {'aux'}, use_global_device_ids=true, to_apply=%region_1.0 | all-reduce | flops 1024 | bytes 8192 | tf_op jit(solution)/shard_map/psum | solution.py:15
Async XLA Ops:
  6.5 140.8 %all-reduce.3.cloned.1.call-start = ((), (), s32[]{:S(2)}) async-start(), calls=%async_computation.1 | async-start | bytes 262144
  47.5 19.3 %copy-start = (u32[128]{0:T(128)S(1)}, u32[128]{0:T(128)}, u32[]{:S(2)}) copy-start(u32[128]{0:T(128)} %constant.3) | copy-start | bytes 1540
Sparse Core Ops, SparseCore 0:
  66.9 80.3 all-reduce.2

commit v2 on v1

v2 whole, which is shorter than its diff:
```python
import functools

import jax
import jax.numpy as jnp
from jax import lax
from jax.experimental import pallas as pl
from jax.experimental.pallas import tpu as pltpu
from jax.sharding import PartitionSpec as P

ROWS = ("vrow", "pair")
ALL = ("vrow", "aux", "pair")
NB = 16
NA = 4
NQ = 15
G = 4
SEND = 64
MIB = 1024 * 1024


def pack_kernel(f_ref, out_ref):
    nq = f_ref.shape[1]
    row = lax.broadcasted_iota(jnp.int32, (SEND, NA * 32), 0)
    col = lax.broadcasted_iota(jnp.int32, (SEND, NA * 32), 1)
    q = (row >> 4) * G + (row & 3)
    a = (row >> 2) & 3
    for j in range(NB):
        base = min(NQ * j // 16 * 16, nq - 32)
        pick = (col == a * 32 + q + (NQ * j - base)) & (q < NQ)
        pick = jnp.where(pick, 1.0, 0.0).astype(jnp.bfloat16)
        window = f_ref[:, base : base + 32, :].reshape(NA * 32, f_ref.shape[2])
        out_ref[j] = jnp.dot(pick, window, preferred_element_type=jnp.float32).astype(jnp.bfloat16)


def ladder_kernel(b_ref, t_ref, out_ref, half_ref, acc_ref):
    p = pl.program_id(0)
    width = b_ref.shape[2]
    rows = b_ref[...].reshape(NB * SEND, width)
    for n in range(0, width, 256):
        m = min(n + 256, width)
        half = jnp.dot(rows, t_ref[0, :, n:m], preferred_element_type=jnp.float32)
        half_ref[:, :, n:m] = half.astype(jnp.bfloat16).reshape(NB, SEND, m - n)

    gram = None
    for g in range(SEND // 16):
        left = half_ref[:, g * 16 : (g + 1) * 16, :].reshape(NB * 16, width)
        right = b_ref[:, g * 16 : (g + 1) * 16, :].reshape(NB * 16, width)
        term = lax.dot_general(left, right, (((1,), (1,)), ((), ())), preferred_element_type=jnp.float32)
        gram = term if gram is None else gram + term

    size = NB * 16
    iota = functools.partial(lax.broadcasted_iota, jnp.int32)
    same = (iota((size, size), 0) & 3) == (iota((size, size), 1) & 3)
    gram = jnp.where(same, gram, 0.0)
    by_b = jnp.where((iota((size, 128), 0) >> 2) + (p // 2) * 64 == iota((size, 128), 1), 1.0, 0.0)
    r, c = iota((128, size), 0), iota((128, size), 1) >> 2
    by_a = jnp.where((c >> 2) * 8 + (p % 2) * 4 + (c & 3) == r, 1.0, 0.0)
    exact = functools.partial(jnp.dot, preferred_element_type=jnp.float32, precision=lax.Precision.HIGHEST)
    part = exact(by_a, exact(gram, by_b))

    @pl.when(p == 0)
    def _():
        acc_ref[...] = part

    @pl.when(p > 0)
    def _():
        acc_ref[...] += part

    @pl.when(p == pl.num_programs(0) - 1)
    def _():
        total = acc_ref[...].reshape(8, 2, 8, 128)
        for x in range(8):
            out_ref[:, x] = total


def sum_kernel(x_ref, out_ref):
    total = jnp.sum(x_ref[...], axis=0)
    for p in range(4):
        out_ref[p] = total[(p % 2) * 4 : (p % 2) * 4 + 4, (p // 2) * 64 : (p // 2) * 64 + 64]


def local(factors, amplitudes):
    width = factors.shape[2]
    npairs = amplitudes.shape[0]
    packed = pl.pallas_call(
        pack_kernel,
        out_shape=jax.ShapeDtypeStruct((NB, SEND, width), jnp.bfloat16),
        compiler_params=pltpu.CompilerParams(vmem_limit_bytes=32 * MIB),
    )(factors)
    mine = lax.all_to_all(packed, ROWS, split_axis=0, concat_axis=0, tiled=True)
    terms = pl.pallas_call(
        ladder_kernel,
        grid=(npairs,),
        in_specs=[
            pl.BlockSpec((NB, SEND, width), lambda p: (0, 0, 0)),
            pl.BlockSpec((1, width, width), lambda p: (p, 0, 0)),
        ],
        out_specs=pl.BlockSpec((8, 8, 2, 8, 128), lambda p: (0, 0, 0, 0, 0)),
        out_shape=jax.ShapeDtypeStruct((8, 8, 2, 8, 128), jnp.float32),
        scratch_shapes=[
            pltpu.VMEM((NB, SEND, width), jnp.bfloat16),
            pltpu.VMEM((128, 128), jnp.float32),
        ],
        compiler_params=pltpu.CompilerParams(vmem_limit_bytes=40 * MIB),
    )(mine, amplitudes)
    terms = lax.all_to_all(terms.reshape(128, 8, 128), ALL, split_axis=0, concat_axis=0, tiled=True)
    return pl.pallas_call(
        sum_kernel,
        out_shape=jax.ShapeDtypeStruct((npairs, NA, NB * NA), jnp.float32),
    )(terms)


def solution(mesh):
    in_specs = (P(ROWS, "aux", None), P())
    out_specs = P(None, ROWS, None)
    return jax.shard_map(local, mesh=mesh, in_specs=in_specs, out_specs=out_specs, check_vma=False)
```

time: 169 us -> 77.7 us (0.46)
  waiting for transfers between devices: 79.3 us -> 0 us
  Pallas kernels: 0 us -> 19.9 us
  matrix products: 19.3 us -> 0 us
  between operations: 14.1 us -> 0.02 us
  blocking collectives: 48.4 us -> 56 us
  local copies, waits for them, and re-layouts: 7.62 us -> 1.55 us
    unnamed x2 -> x0, waiting for transfers between devices: 79.3 us -> none
    all_to_all x1 -> x2, blocking collectives: 34.6 us -> 56 us  [the longest x1 36.1 us: local(): mine = lax.all_to_all(packed, ROWS, split_axis=0, concat_axis=0, tiled=True)]
    pallas_call x0 -> x3, Pallas kernels: none -> 19.9 us  [the longest x1 17.4 us: local(): pl.pallas_call(ladder_kernel, grid=(npairs,), in_specs=[pl.BlockSpec((NB,...]
    dot_general x1 -> x0, matrix products: 19.3 us -> none  [local(): jnp.einsum('paqd,bqd->pab', half, mine, preferred_element_type=jnp.float32)]
    psum x1 -> x0, blocking collectives: 13.8 us -> none  [local(): return lax.psum(terms, 'aux')]
    all_to_all x2 -> x0, local copies, waits for them, and re-layouts: 3.24 us -> none  [local(): lax.all_to_all(factors, ROWS, split_axis=1, concat_axis=0, tiled=True)]
    unnamed x5 -> x4, local copies, waits for them, and re-layouts: 4.37 us -> 1.55 us
  transfers between devices with their start and end apart: 1 -> 0, of which waited for: 1 -> 0; matrix products, arithmetic and copies ran while one was open for 0% -> 0% of each run, Pallas kernels for 0% -> 0%
where the time goes in v2:
time: 77.7 us; the launch traced here: 77.5 us
  blocking collectives  56 us (72%)
  Pallas kernels  19.9 us (26%)
  local copies, waits for them, and re-layouts  1.55 us (2%)
    all_to_all x1, blocking collectives, local(): mine = lax.all_to_all(packed, ROWS, split_axis=0, concat_axis=0, tiled=True)  36.1 us
    all_to_all x1, blocking collectives, local(): lax.all_to_all(terms.reshape(128, 8, 128), ALL, split_axis=0, concat_axis...  19.9 us
    pallas_call x1, Pallas kernels, local(): pl.pallas_call(ladder_kernel, grid=(npairs,), in_specs=[pl.BlockSpec((NB,...  17.4 us
    pallas_call x1, Pallas kernels, local(): pl.pallas_call(sum_kernel, out_shape=jax.ShapeDtypeStruct((npairs, NA, NB...  1.84 us

profile of v2, /device:TPU:0, one launch (start us, length us, event | category | flops | bytes accessed | tf_op | source)
XLA Modules:
  0.0 77.5 jit_solution(11996662346255374748)
XLA Ops:
  0.0 0.0 copy-start.1
  0.0 1.5 %copy-done.1 = bf16[4,240,960]{2,1,0:T(8,128)(2,1)S(1)} copy-done((bf16[4,240,960]{2,1,0:T(8,128)(2,1)S(1)}, bf16[4,240,960]{2,1,0:T(8,128)(2,1)}, u32[]{:S(2)}) %copy-start.1) | copy-done | bytes 1843224
  1.5 0.0 copy-start
  1.5 0.7 shard_map.28
  2.3 36.1 %all_to_all.10.b_ref = bf16[16,64,960]{2,1,0:T(8,128)(2,1)S(1)} all-to-all(bf16[16,64,960]{2,1,0:T(8,128)(2,1)S(1)} %shard_map.28), channel_id=1, replica_groups=mesh['vrow'=8,'aux'=8,'pair'=2] {'vrow','pair'}, dimensions={0} | all-to-all | bytes 3932160 | tf_op jit(solution)/shard_map/all_to_all | solution.py:89
  38.4 0.0 copy-done
  38.4 17.4 %shard_map.29 = f32[8,8,2,8,128]{4,3,2,1,0:T(8,128)S(1)} custom-call(bf16[16,64,960]{2,1,0:T(8,128)(2,1)S(1)} %all_to_all.10.b_ref, bf16[4,960,960]{2,1,0:T(8,128)(2,1)S(1)} %copy-done), custom_call_target="tpu_custom_call" | custom-call | tf_op jit(solution)/shard_map/pallas_call | solution.py:90
  55.7 19.9 %all_to_all.11.x_ref = f32[128,8,128]{2,1,0:T(8,128)} all-to-all(f32[128,8,128]{2,1,0:T(8,128)S(1)} %bitcast.1), channel_id=1, replica_groups=mesh['vrow'=8,'aux'=8,'pair'=2] {'vrow','aux','pair'}, dimensions={0} | all-to-all | bytes 1048576 | tf_op jit(solution)/shard_map/all_to_all | solution.py:105
  75.6 1.8 %shard_map.30 = f32[4,4,64]{2,1,0:T(4,128)} custom-call(f32[128,8,128]{2,1,0:T(8,128)} %all_to_all.11.x_ref), custom_call_target="tpu_custom_call" | custom-call | tf_op jit(solution)/shard_map/pallas_call | solution.py:106
Async XLA Ops:
  0.0 1.5 %copy-start.1 = (bf16[4,240,960]{2,1,0:T(8,128)(2,1)S(1)}, bf16[4,240,960]{2,1,0:T(8,128)(2,1)}, u32[]{:S(2)}) copy-start(bf16[4,240,960]{2,1,0:T(8,128)(2,1)} %f_ref.1) | copy-start | bytes 5529604
  1.5 36.8 %copy-start = (bf16[4,960,960]{2,1,0:T(8,128)(2,1)S(1)}, bf16[4,960,960]{2,1,0:T(8,128)(2,1)}, u32[]{:S(2)}) copy-start(bf16[4,960,960]{2,1,0:T(8,128)(2,1)} %t_ref.1) | copy-start | bytes 22118404

commit v3 on v1

v3 whole, which is shorter than its diff:
```python
import functools

import jax
import jax.numpy as jnp
from jax import lax
from jax.experimental import pallas as pl
from jax.experimental.pallas import tpu as pltpu
from jax.sharding import PartitionSpec as P

ROWS = ("vrow", "pair")
ALL = ("vrow", "aux", "pair")
V = 960
NB = 16
NA = 4
NQ = 15
G = 4
SEND = 64
MAIN = 896
TILES = MAIN // 128
BLOCK = TILES * SEND + SEND // 2
MIB = 1024 * 1024

iota = functools.partial(lax.broadcasted_iota, jnp.int32)


def pack_kernel(f_ref, out_ref):
    nq = f_ref.shape[1]
    row, col = iota((SEND, NA * 32), 0), iota((SEND, NA * 32), 1)
    q, a = row >> 2, row & 3
    for j in range(NB):
        base = min(NQ * j // 16 * 16, nq - 32)
        pick = (col == a * 32 + q + (NQ * j - base)) & (q < NQ)
        pick = jnp.where(pick, 1.0, 0.0).astype(jnp.bfloat16)
        window = f_ref[:, base : base + 32, :].reshape(NA * 32, V)
        rows = jnp.dot(pick, window, preferred_element_type=jnp.float32).astype(jnp.bfloat16)
        for k in range(TILES):
            out_ref[j, k * SEND : (k + 1) * SEND, :] = rows[:, k * 128 : (k + 1) * 128]
        tails = [rows[: SEND // 2, MAIN:], rows[SEND // 2 :, MAIN:]]
        out_ref[j, TILES * SEND :, :] = jnp.concatenate(tails, axis=1)


def split(x, terms):
    out = []
    for _ in range(terms):
        high = x.astype(jnp.bfloat16)
        out.append(high)
        x = x - high.astype(jnp.float32)
    return out


def ladder_kernel(b_ref, t_ref, out_ref, half_ref, gram_ref, tail_ref):
    npairs = t_ref.shape[0]
    for i in range(npairs // 2):
        tails = [t_ref[2 * i, :, MAIN:], t_ref[2 * i + 1, :, MAIN:]]
        tail_ref[:, i * 128 : (i + 1) * 128] = jnp.concatenate(tails, axis=1)

    def columns(n):
        tiles = []
        for i in (2 * n, 2 * n + 1):
            if i < npairs * TILES:
                tiles.append(t_ref[i // TILES, :, i % TILES * 128 : i % TILES * 128 + 128])
            else:
                i -= npairs * TILES
                tiles.append(tail_ref[:, i * 128 : (i + 1) * 128])
        return jnp.concatenate(tiles, axis=1)

    size = NB * 16
    lane = iota((size, 128), 1)
    for g in range(SEND // 16):
        def block(start):
            return b_ref[:, start : start + 16, :].reshape(size, 128)

        main = jnp.concatenate([block(k * SEND + g * 16) for k in range(TILES)], axis=1)
        low = block(TILES * SEND + g % 2 * 16)
        high = jnp.concatenate([low[:, 64:], low[:, :64]], axis=1)
        if g >= 2:
            low, high = high, low
        low = jnp.where(lane < 64, low, jnp.zeros_like(low))
        high = jnp.where(lane < 64, jnp.zeros_like(high), high)

        rows = jnp.concatenate([main, low[:, :64]], axis=1)
        for n in range(npairs * V // 256):
            half = jnp.dot(rows, columns(n), preferred_element_type=jnp.float32)
            half_ref[g, :, n * 256 : (n + 1) * 256] = half.astype(jnp.bfloat16)

        right = [jnp.concatenate([main, low], axis=1), jnp.concatenate([main, high], axis=1)]
        for p in range(npairs):
            tail = npairs * MAIN + p // 2 * 128
            left = [half_ref[g, :, p * MAIN : (p + 1) * MAIN], half_ref[g, :, tail : tail + 128]]
            term = lax.dot_general(
                jnp.concatenate(left, axis=1),
                right[p % 2],
                (((1,), (1,)), ((), ())),
                preferred_element_type=jnp.float32,
            )
            if g == 0:
                gram_ref[p] = term
            else:
                gram_ref[p] += term

    same = (iota((size, size), 0) >> 2 & 3) == (iota((size, size), 1) >> 2 & 3)
    sums = []
    for p in range(npairs):
        s = jnp.where(same, gram_ref[p], 0.0).reshape(NB, 2, 8, size)
        s = s[:, 0] + s[:, 1]
        sums.append(s + pltpu.roll(s, 4, 1))
    first = iota((NB, 8, size), 1) < 4
    pairs = [jnp.where(first, sums[p], sums[p + 1]).reshape(NB * 8, size) for p in range(0, npairs, 2)]
    r, l = iota((2 * size, 128), 0), iota((2 * size, 128), 1)
    pick = jnp.where(l == (r >> 8) * 64 + (r >> 4 & 15) * 4 + (r & 3), 1.0, 0.0).astype(jnp.bfloat16)
    total = jnp.zeros((NB * 8, 128), jnp.float32)
    for term in split(jnp.concatenate(pairs, axis=1), 3):
        total += jnp.dot(term, pick, preferred_element_type=jnp.float32)
    total = total.reshape(8, 2, 8, 128)
    for x in range(8):
        out_ref[:, x] = total


def sum_kernel(x_ref, out_ref):
    total = jnp.sum(x_ref[...], axis=0)
    for p in range(4):
        out_ref[p] = total[(p % 2) * 4 : (p % 2) * 4 + 4, (p // 2) * 64 : (p // 2) * 64 + 64]


def local(factors, amplitudes):
    npairs = amplitudes.shape[0]
    vmem = pl.BlockSpec(memory_space=pltpu.VMEM)
    packed = pl.pallas_call(
        pack_kernel,
        in_specs=[vmem],
        out_specs=vmem,
        out_shape=jax.ShapeDtypeStruct((NB, BLOCK, 128), jnp.bfloat16),
        compiler_params=pltpu.CompilerParams(vmem_limit_bytes=32 * MIB),
    )(factors)
    mine = lax.all_to_all(packed, ROWS, split_axis=0, concat_axis=0, tiled=True)
    size = NB * 16
    terms = pl.pallas_call(
        ladder_kernel,
        in_specs=[vmem, vmem],
        out_specs=vmem,
        out_shape=jax.ShapeDtypeStruct((8, 8, 2, 8, 128), jnp.float32),
        scratch_shapes=[
            pltpu.VMEM((SEND // 16, size, npairs * V), jnp.bfloat16),
            pltpu.VMEM((npairs, size, size), jnp.float32),
            pltpu.VMEM((V, npairs * 64), jnp.bfloat16),
        ],
        compiler_params=pltpu.CompilerParams(vmem_limit_bytes=40 * MIB),
    )(mine, amplitudes)
    terms = lax.all_to_all(terms.reshape(128, 8, 128), ALL, split_axis=0, concat_axis=0, tiled=True)
    return pl.pallas_call(
        sum_kernel,
        in_specs=[vmem],
        out_specs=vmem,
        out_shape=jax.ShapeDtypeStruct((npairs, NA, NB * NA), jnp.float32),
    )(terms)


def solution(mesh):
    in_specs = (P(ROWS, "aux", None), P())
    out_specs = P(None, ROWS, None)
    return jax.shard_map(local, mesh=mesh, in_specs=in_specs, out_specs=out_specs, check_vma=False)
```

time: 169 us -> 72.9 us (0.43)
  waiting for transfers between devices: 79.3 us -> 0 us
  matrix products: 19.3 us -> 0 us
  between operations: 14.1 us -> 0.01 us
  Pallas kernels: 0 us -> 13.5 us
  blocking collectives: 48.4 us -> 54.3 us
  local copies, waits for them, and re-layouts: 7.62 us -> 4.78 us
    unnamed x2 -> x0, waiting for transfers between devices: 79.3 us -> none
    all_to_all x1 -> x2, blocking collectives: 34.6 us -> 54.3 us  [the longest x1 34.6 us: local(): mine = lax.all_to_all(packed, ROWS, split_axis=0, concat_axis=0, tiled=True)]
    dot_general x1 -> x0, matrix products: 19.3 us -> none  [local(): jnp.einsum('paqd,bqd->pab', half, mine, preferred_element_type=jnp.float32)]
    psum x1 -> x0, blocking collectives: 13.8 us -> none  [local(): return lax.psum(terms, 'aux')]
    pallas_call x0 -> x3, Pallas kernels: none -> 13.5 us  [the longest x1 10.9 us: local(): pl.pallas_call(ladder_kernel, in_specs=[vmem, vmem], out_specs=vmem, out_...]
    all_to_all x2 -> x0, local copies, waits for them, and re-layouts: 3.24 us -> none  [local(): lax.all_to_all(factors, ROWS, split_axis=1, concat_axis=0, tiled=True)]
    unnamed x5 -> x4, local copies, waits for them, and re-layouts: 4.37 us -> 4.78 us
  transfers between devices with their start and end apart: 1 -> 0, of which waited for: 1 -> 0; matrix products, arithmetic and copies ran while one was open for 0% -> 0% of each run, Pallas kernels for 0% -> 0%
where the time goes in v3:
time: 72.9 us; the launch traced here: 72.6 us
  blocking collectives  54.3 us (74%)
  Pallas kernels  13.5 us (19%)
  local copies, waits for them, and re-layouts  4.78 us (7%)
    all_to_all x1, blocking collectives, local(): mine = lax.all_to_all(packed, ROWS, split_axis=0, concat_axis=0, tiled=True)  34.6 us
    all_to_all x1, blocking collectives, local(): lax.all_to_all(terms.reshape(128, 8, 128), ALL, split_axis=0, concat_axis...  19.7 us
    pallas_call x1, Pallas kernels, local(): pl.pallas_call(ladder_kernel, in_specs=[vmem, vmem], out_specs=vmem, out_...  10.9 us
    unnamed x4, local copies, waits for them, and re-layouts  4.78 us
    pallas_call x1, Pallas kernels, local(): pl.pallas_call(sum_kernel, in_specs=[vmem], out_specs=vmem, out_shape=jax...  1.84 us

profile of v3, /device:TPU:0, one launch (start us, length us, event | category | flops | bytes accessed | tf_op | source)
XLA Modules:
  0.0 72.6 jit_solution(5888801700612141345)
XLA Ops:
  0.0 0.0 copy-start.1
  0.0 1.5 %copy-done.1 = bf16[4,240,960]{2,1,0:T(8,128)(2,1)S(1)} copy-done((bf16[4,240,960]{2,1,0:T(8,128)(2,1)S(1)}, bf16[4,240,960]{2,1,0:T(8,128)(2,1)}, u32[]{:S(2)}) %copy-start.1) | copy-done | bytes 1843224
  1.5 0.8 %shard_map.28 = bf16[16,480,128]{2,1,0:T(8,128)(2,1)S(1)} custom-call(bf16[4,240,960]{2,1,0:T(8,128)(2,1)S(1)} %copy-done.1), custom_call_target="tpu_custom_call" | custom-call | tf_op jit(solution)/shard_map/pallas_call | solution.py:128
  2.3 34.6 %all_to_all.10.b_ref = bf16[16,480,128]{2,1,0:T(8,128)(2,1)S(1)} all-to-all(bf16[16,480,128]{2,1,0:T(8,128)(2,1)S(1)} %shard_map.28), channel_id=1, replica_groups=mesh['vrow'=8,'aux'=8,'pair'=2] {'vrow','pair'}, dimensions={0} | all-to-all | bytes 3932160 | tf_op jit(solution)/shard_map/all_to_all | solution.py:135
  36.9 0.0 copy-start
  36.9 3.2 %copy-done = bf16[4,960,960]{2,1,0:T(8,128)(2,1)S(1)} copy-done((bf16[4,960,960]{2,1,0:T(8,128)(2,1)S(1)}, bf16[4,960,960]{2,1,0:T(8,128)(2,1)}, u32[]{:S(2)}) %copy-start) | copy-done | bytes 7372824
  40.2 10.9 %shard_map.29 = f32[8,8,2,8,128]{4,3,2,1,0:T(8,128)S(1)} custom-call(bf16[16,480,128]{2,1,0:T(8,128)(2,1)S(1)} %all_to_all.10.b_ref, bf16[4,960,960]{2,1,0:T(8,128)(2,1)S(1)} %copy-done), custom_call_target="tpu_custom_call" | custom-call | tf_op jit(solution)/shard_map/pallas_call | solution.py:137
  51.1 19.7 %all_to_all.11.x_ref = f32[128,8,128]{2,1,0:T(8,128)} all-to-all(f32[128,8,128]{2,1,0:T(8,128)S(1)} %bitcast.1), channel_id=1, replica_groups=mesh['vrow'=8,'aux'=8,'pair'=2] {'vrow','aux','pair'}, dimensions={0} | all-to-all | bytes 1048576 | tf_op jit(solution)/shard_map/all_to_all | solution.py:149
  70.8 1.8 %shard_map.30 = f32[4,4,64]{2,1,0:T(4,128)} custom-call(f32[128,8,128]{2,1,0:T(8,128)} %all_to_all.11.x_ref), custom_call_target="tpu_custom_call" | custom-call | tf_op jit(solution)/shard_map/pallas_call | solution.py:150
Async XLA Ops:
  0.0 1.5 %copy-start.1 = (bf16[4,240,960]{2,1,0:T(8,128)(2,1)S(1)}, bf16[4,240,960]{2,1,0:T(8,128)(2,1)}, u32[]{:S(2)}) copy-start(bf16[4,240,960]{2,1,0:T(8,128)(2,1)} %f_ref.1) | copy-start | bytes 5529604
  36.9 3.2 %copy-start = (bf16[4,960,960]{2,1,0:T(8,128)(2,1)S(1)}, bf16[4,960,960]{2,1,0:T(8,128)(2,1)}, u32[]{:S(2)}) copy-start(bf16[4,960,960]{2,1,0:T(8,128)(2,1)} %t_ref.1) | copy-start | bytes 22118404

commit v4 on v3

--- a/solution.py
+++ b/solution.py
@@ -130,7 +130,8 @@
         in_specs=[vmem],
         out_specs=vmem,
         out_shape=jax.ShapeDtypeStruct((NB, BLOCK, 128), jnp.bfloat16),
-        compiler_params=pltpu.CompilerParams(vmem_limit_bytes=32 * MIB),
+        compiler_params=pltpu.CompilerParams(vmem_limit_bytes=10 * MIB),
+        cost_estimate=pl.CostEstimate(flops=2 * 10**10, bytes_accessed=4 * 10**7, transcendentals=0),
     )(factors)
     mine = lax.all_to_all(packed, ROWS, split_axis=0, concat_axis=0, tiled=True)
     size = NB * 16
@@ -144,15 +145,11 @@
             pltpu.VMEM((npairs, size, size), jnp.float32),
             pltpu.VMEM((V, npairs * 64), jnp.bfloat16),
         ],
-        compiler_params=pltpu.CompilerParams(vmem_limit_bytes=40 * MIB),
+        compiler_params=pltpu.CompilerParams(vmem_limit_bytes=28 * MIB),
     )(mine, amplitudes)
     terms = lax.all_to_all(terms.reshape(128, 8, 128), ALL, split_axis=0, concat_axis=0, tiled=True)
-    return pl.pallas_call(
-        sum_kernel,
-        in_specs=[vmem],
-        out_specs=vmem,
-        out_shape=jax.ShapeDtypeStruct((npairs, NA, NB * NA), jnp.float32),
-    )(terms)
+    total = jnp.sum(terms, axis=0).reshape(2, NA, npairs // 2, NB * NA)
+    return jnp.transpose(total, (2, 0, 1, 3)).reshape(npairs, NA, NB * NA)
 
 
 def solution(mesh):

time: 72.9 us -> 68.7 us (0.942)
  local copies, waits for them, and re-layouts: 4.78 us -> 2.23 us
  Pallas kernels: 13.5 us -> 11.7 us
    unnamed x4, local copies, waits for them, and re-layouts: 4.78 us -> 1.55 us
    pallas_call x1 -> x0, Pallas kernels: 1.84 us -> none  [local(): pl.pallas_call(sum_kernel, in_specs=[vmem], out_specs=vmem, out_shape=jax...]
where the time goes in v4:
time: 68.7 us; the launch traced here: 68.5 us
  blocking collectives  54.5 us (79%)
  Pallas kernels  11.7 us (17%)
  local copies, waits for them, and re-layouts  2.23 us (3%)
    all_to_all x1, blocking collectives, local(): mine = lax.all_to_all(packed, ROWS, split_axis=0, concat_axis=0, tiled=True)  34.9 us
    all_to_all x1, blocking collectives, local(): lax.all_to_all(terms.reshape(128, 8, 128), ALL, split_axis=0, concat_axis...  19.6 us
    pallas_call x1, Pallas kernels, local(): pl.pallas_call(ladder_kernel, in_specs=[vmem, vmem], out_specs=vmem, out_...  10.9 us
    unnamed x4, local copies, waits for them, and re-layouts  1.55 us

profile of v4, /device:TPU:0, one launch (start us, length us, event | category | flops | bytes accessed | tf_op | source)
XLA Modules:
  0.0 68.5 jit_solution(9790997213115059126)
XLA Ops:
  0.0 0.0 copy-start.1
  0.0 1.5 %copy-done.1 = bf16[4,240,960]{2,1,0:T(8,128)(2,1)S(1)} copy-done((bf16[4,240,960]{2,1,0:T(8,128)(2,1)S(1)}, bf16[4,240,960]{2,1,0:T(8,128)(2,1)}, u32[]{:S(2)}) %copy-start.1) | copy-done | bytes 1843224
  1.5 0.0 copy-start
  1.5 0.8 %shard_map.28 = bf16[16,480,128]{2,1,0:T(8,128)(2,1)S(1)} custom-call(bf16[4,240,960]{2,1,0:T(8,128)(2,1)S(1)} %copy-done.1), custom_call_target="tpu_custom_call" | custom-call | flops 20000000000 | bytes 40000000 | tf_op jit(solution)/shard_map/pallas_call | solution.py:128
  2.3 34.9 %all_to_all.10.b_ref = bf16[16,480,128]{2,1,0:T(8,128)(2,1)S(1)} all-to-all(bf16[16,480,128]{2,1,0:T(8,128)(2,1)S(1)} %shard_map.28), channel_id=1, replica_groups=mesh['vrow'=8,'aux'=8,'pair'=2] {'vrow','pair'}, dimensions={0} | all-to-all | bytes 3932160 | tf_op jit(solution)/shard_map/all_to_all | solution.py:136
  37.2 0.0 copy-done
  37.2 10.9 %shard_map.29 = f32[8,8,2,8,128]{4,3,2,1,0:T(8,128)S(1)} custom-call(bf16[16,480,128]{2,1,0:T(8,128)(2,1)S(1)} %all_to_all.10.b_ref, bf16[4,960,960]{2,1,0:T(8,128)(2,1)S(1)} %copy-done), custom_call_target="tpu_custom_call" | custom-call | tf_op jit(solution)/shard_map/pallas_call | solution.py:138
  48.1 19.6 %all_to_all.11 = f32[128,8,128]{2,1,0:T(8,128)S(1)} all-to-all(f32[128,8,128]{2,1,0:T(8,128)S(1)} %bitcast.3), channel_id=1, replica_groups=mesh['vrow'=8,'aux'=8,'pair'=2] {'vrow','aux','pair'}, dimensions={0} | all-to-all | bytes 1048576 | tf_op jit(solution)/shard_map/all_to_all | solution.py:150
  67.7 0.1 reduce_sum.9
  67.8 0.1 reshape.10
  67.9 0.6 copy.3
Async XLA Ops:
  0.0 1.5 %copy-start.1 = (bf16[4,240,960]{2,1,0:T(8,128)(2,1)S(1)}, bf16[4,240,960]{2,1,0:T(8,128)(2,1)}, u32[]{:S(2)}) copy-start(bf16[4,240,960]{2,1,0:T(8,128)(2,1)} %f_ref.1) | copy-start | bytes 5529604
  1.5 35.6 %copy-start = (bf16[4,960,960]{2,1,0:T(8,128)(2,1)S(1)}, bf16[4,960,960]{2,1,0:T(8,128)(2,1)}, u32[]{:S(2)}) copy-start(bf16[4,960,960]{2,1,0:T(8,128)(2,1)} %t_ref.1) | copy-start | bytes 22118404

commit v5 on v4

--- a/solution.py
+++ b/solution.py
@@ -14,10 +14,15 @@
 NA = 4
 NQ = 15
 G = 4
-SEND = 64
 MAIN = 896
 TILES = MAIN // 128
-BLOCK = TILES * SEND + SEND // 2
+FULL = 3
+HEAD = FULL * NA * G
+TAIL = TILES * HEAD
+LAST = TAIL + 2 * 16
+SPREAD = 5
+LAST_TILES = [k for k in range(TILES) if k != SPREAD]
+BLOCK = LAST + len(LAST_TILES) * 16
 MIB = 1024 * 1024
 
 iota = functools.partial(lax.broadcasted_iota, jnp.int32)
@@ -25,18 +30,30 @@
 
 def pack_kernel(f_ref, out_ref):
     nq = f_ref.shape[1]
-    row, col = iota((SEND, NA * 32), 0), iota((SEND, NA * 32), 1)
-    q, a = row >> 2, row & 3
+    shape = (HEAD + 3 * 16, NA * 32)
+    row, col = iota(shape, 0), iota(shape, 1)
+    slot, a = row >> 2 & 3, row & 3
+    q = jnp.where(row < HEAD, row >> 2, FULL * G + jnp.where(slot == 3, (row - HEAD) >> 4, slot))
+    spread = iota((16, 128), 0) >= 3 * NA
     for j in range(NB):
         base = min(NQ * j // 16 * 16, nq - 32)
-        pick = (col == a * 32 + q + (NQ * j - base)) & (q < NQ)
-        pick = jnp.where(pick, 1.0, 0.0).astype(jnp.bfloat16)
+        pick = jnp.where(col == a * 32 + q + (NQ * j - base), 1.0, 0.0).astype(jnp.bfloat16)
         window = f_ref[:, base : base + 32, :].reshape(NA * 32, V)
         rows = jnp.dot(pick, window, preferred_element_type=jnp.float32).astype(jnp.bfloat16)
+
+        def tile(start, k):
+            return rows[start : start + 16, k * 128 : (k + 1) * 128]
+
         for k in range(TILES):
-            out_ref[j, k * SEND : (k + 1) * SEND, :] = rows[:, k * 128 : (k + 1) * 128]
-        tails = [rows[: SEND // 2, MAIN:], rows[SEND // 2 :, MAIN:]]
-        out_ref[j, TILES * SEND :, :] = jnp.concatenate(tails, axis=1)
+            out_ref[j, k * HEAD : (k + 1) * HEAD, :] = rows[:HEAD, k * 128 : (k + 1) * 128]
+        for i in range(2):
+            tails = [rows[32 * i : 32 * i + 16, MAIN:], rows[32 * i + 16 : 32 * i + 32, MAIN:]]
+            out_ref[j, TAIL + 16 * i : TAIL + 16 * i + 16, :] = jnp.concatenate(tails, axis=1)
+        for i, k in enumerate(LAST_TILES):
+            last = tile(HEAD, k)
+            if i < 3:
+                last = jnp.where(spread, tile(HEAD + 16 * i, SPREAD), last)
+            out_ref[j, LAST + 16 * i : LAST + 16 * i + 16, :] = last
 
 
 def split(x, terms):
@@ -48,7 +65,7 @@
     return out
 
 
-def ladder_kernel(b_ref, t_ref, out_ref, half_ref, gram_ref, tail_ref):
+def ladder_kernel(b_ref, t_ref, out_ref, half_ref, gram_ref, last_ref, tail_ref):
     npairs = t_ref.shape[0]
     for i in range(npairs // 2):
         tails = [t_ref[2 * i, :, MAIN:], t_ref[2 * i + 1, :, MAIN:]]
@@ -65,28 +82,50 @@
         return jnp.concatenate(tiles, axis=1)
 
     size = NB * 16
-    lane = iota((size, 128), 1)
-    for g in range(SEND // 16):
-        def block(start):
-            return b_ref[:, start : start + 16, :].reshape(size, 128)
-
-        main = jnp.concatenate([block(k * SEND + g * 16) for k in range(TILES)], axis=1)
-        low = block(TILES * SEND + g % 2 * 16)
+    nlast = 3 * NB * NA
+
+    def block(start):
+        return b_ref[:, start : start + 16, :].reshape(size, 128)
+
+    def last_group():
+        r, c = iota((nlast, size), 0), iota((nlast, size), 1)
+        put = jnp.where(c == (r >> 2 & 15) * 16 + (r >> 6) * 4 + (r & 3), 1.0, 0.0).astype(jnp.bfloat16)
+        r, c = iota((NB * NA, size), 0), iota((NB * NA, size), 1)
+        get = jnp.where(c == (r >> 2) * 16 + 12 + (r & 3), 1.0, 0.0).astype(jnp.bfloat16)
+
+        def move(matrix, x):
+            return jnp.dot(matrix, x, preferred_element_type=jnp.float32).astype(jnp.bfloat16)
+
+        tiles = [block(LAST + 16 * i) for i in range(len(LAST_TILES))]
+        spread = [move(get, tiles[i]) for i in range(3)]
+        moved = move(put, jnp.concatenate(tiles + [block(TAIL + 16)], axis=1))
+        moved = [moved[:, i * 128 : (i + 1) * 128] for i in range(len(LAST_TILES) + 1)]
+        moved.insert(SPREAD, jnp.concatenate(spread, axis=0))
+        return jnp.concatenate(moved[:TILES], axis=1), moved[TILES]
+
+    for g in range(FULL + 1):
+        if g < FULL:
+            main = jnp.concatenate([block(k * HEAD + g * 16) for k in range(TILES)], axis=1)
+            low = block(TAIL + g // 2 * 16)
+        else:
+            main, low = last_group()
+        nrows = main.shape[0]
         high = jnp.concatenate([low[:, 64:], low[:, :64]], axis=1)
-        if g >= 2:
+        if g % 2:
             low, high = high, low
-        low = jnp.where(lane < 64, low, jnp.zeros_like(low))
-        high = jnp.where(lane < 64, jnp.zeros_like(high), high)
+        first = iota((nrows, 128), 1) < 64
+        low = jnp.where(first, low, jnp.zeros_like(low))
+        high = jnp.where(first, jnp.zeros_like(high), high)
 
         rows = jnp.concatenate([main, low[:, :64]], axis=1)
         for n in range(npairs * V // 256):
             half = jnp.dot(rows, columns(n), preferred_element_type=jnp.float32)
-            half_ref[g, :, n * 256 : (n + 1) * 256] = half.astype(jnp.bfloat16)
+            half_ref[g, :nrows, n * 256 : (n + 1) * 256] = half.astype(jnp.bfloat16)
 
         right = [jnp.concatenate([main, low], axis=1), jnp.concatenate([main, high], axis=1)]
         for p in range(npairs):
             tail = npairs * MAIN + p // 2 * 128
-            left = [half_ref[g, :, p * MAIN : (p + 1) * MAIN], half_ref[g, :, tail : tail + 128]]
+            left = [half_ref[g, :nrows, p * MAIN : (p + 1) * MAIN], half_ref[g, :nrows, tail : tail + 128]]
             term = lax.dot_general(
                 jnp.concatenate(left, axis=1),
                 right[p % 2],
@@ -95,8 +134,11 @@
             )
             if g == 0:
                 gram_ref[p] = term
+            elif g < FULL:
+                gram_ref[p] += term
             else:
-                gram_ref[p] += term
+                n = NB * NA
+                last_ref[p] = term[:n, :n] + term[n : 2 * n, n : 2 * n] + term[2 * n :, 2 * n :]
 
     same = (iota((size, size), 0) >> 2 & 3) == (iota((size, size), 1) >> 2 & 3)
     sums = []
@@ -111,15 +153,14 @@
     total = jnp.zeros((NB * 8, 128), jnp.float32)
     for term in split(jnp.concatenate(pairs, axis=1), 3):
         total += jnp.dot(term, pick, preferred_element_type=jnp.float32)
-    total = total.reshape(8, 2, 8, 128)
-    for x in range(8):
-        out_ref[:, x] = total
-
-
-def sum_kernel(x_ref, out_ref):
-    total = jnp.sum(x_ref[...], axis=0)
-    for p in range(4):
-        out_ref[p] = total[(p % 2) * 4 : (p % 2) * 4 + 4, (p // 2) * 64 : (p // 2) * 64 + 64]
+    total = total.reshape(NB // 2, 2, 8, 128)
+
+    even, odd = [
+        jnp.concatenate([last_ref[p], last_ref[p + 2]], axis=1).reshape(NB // 2, 8, 128) for p in range(2)
+    ]
+    first = iota((NB // 2, 8, 128), 1) < 4
+    out_ref[:, 0] = total[:, 0] + jnp.where(first, even, pltpu.roll(odd, 4, 1))
+    out_ref[:, 1] = total[:, 1] + jnp.where(first, pltpu.roll(even, 4, 1), odd)
 
 
 def local(factors, amplitudes):
@@ -139,15 +180,19 @@
         ladder_kernel,
         in_specs=[vmem, vmem],
         out_specs=vmem,
-        out_shape=jax.ShapeDtypeStruct((8, 8, 2, 8, 128), jnp.float32),
+        out_shape=jax.ShapeDtypeStruct((NB // 2, 2, 8, 128), jnp.float32),
         scratch_shapes=[
-            pltpu.VMEM((SEND // 16, size, npairs * V), jnp.bfloat16),
+            pltpu.VMEM((FULL + 1, size, npairs * V), jnp.bfloat16),
             pltpu.VMEM((npairs, size, size), jnp.float32),
+            pltpu.VMEM((npairs, NB * NA, NB * NA), jnp.float32),
             pltpu.VMEM((V, npairs * 64), jnp.bfloat16),
         ],
         compiler_params=pltpu.CompilerParams(vmem_limit_bytes=28 * MIB),
     )(mine, amplitudes)
-    terms = lax.all_to_all(terms.reshape(128, 8, 128), ALL, split_axis=0, concat_axis=0, tiled=True)
+    terms = terms + lax.ppermute(terms, "aux", [(i, i ^ 1) for i in range(8)])
+    terms = jnp.broadcast_to(terms[:, None], (8, 4, 2, 8, 128)).reshape(64, 8, 128)
+    groups = [[(v * 8 + 2 * x + c) * 2 + p for v in range(8) for x in range(4) for p in range(2)] for c in range(2)]
+    terms = lax.all_to_all(terms, ALL, split_axis=0, concat_axis=0, tiled=True, axis_index_groups=groups)
     total = jnp.sum(terms, axis=0).reshape(2, NA, npairs // 2, NB * NA)
     return jnp.transpose(total, (2, 0, 1, 3)).reshape(npairs, NA, NB * NA)
 

time: 68.7 us -> 67.2 us (0.978)
  blocking collectives: 54.5 us -> 51.8 us
  waiting for transfers between devices: 0 us -> 1.24 us
    all_to_all x1, blocking collectives: 19.6 us -> 17.5 us  [local(): lax.all_to_all(terms, ALL, split_axis=0, concat_axis=0, tiled=True, axis_...]
    ppermute x0 -> x1, waiting for transfers between devices: none -> 1.24 us  [local(): terms = terms + lax.ppermute(terms, 'aux', [(i, i ^ 1) for i in range(8)])]
  transfers between devices with their start and end apart: 0 -> 1, of which waited for: 0 -> 1; matrix products, arithmetic and copies ran while one was open for 0% -> 0% of each run, Pallas kernels for 0% -> 0%
where the time goes in v5:
time: 67.2 us; the launch traced here: 67 us
  blocking collectives  51.8 us (77%)
  Pallas kernels  11.5 us (17%)
  local copies, waits for them, and re-layouts  2.25 us (3%)
  waiting for transfers between devices  1.24 us (2%)
    all_to_all x1, blocking collectives, local(): mine = lax.all_to_all(packed, ROWS, split_axis=0, concat_axis=0, tiled=True)  34.3 us
    all_to_all x1, blocking collectives, local(): lax.all_to_all(terms, ALL, split_axis=0, concat_axis=0, tiled=True, axis_...  17.5 us
    pallas_call x1, Pallas kernels, local(): pl.pallas_call(ladder_kernel, in_specs=[vmem, vmem], out_specs=vmem, out_...  10.5 us
    unnamed x4, local copies, waits for them, and re-layouts  1.55 us
  transfers between devices with their start and end apart: 1, of which 1 were waited for; matrix products, arithmetic and copies ran while one was open for 0% of the time, Pallas kernels for 0%

profile of v5, /device:TPU:0, one launch (start us, length us, event | category | flops | bytes accessed | tf_op | source)
XLA Modules:
  0.0 67.0 jit_solution(4584045363910679784)
XLA Ops:
  0.0 0.0 copy-start.1
  0.0 1.5 %copy-done.1 = bf16[4,240,960]{2,1,0:T(8,128)(2,1)S(1)} copy-done((bf16[4,240,960]{2,1,0:T(8,128)(2,1)S(1)}, bf16[4,240,960]{2,1,0:T(8,128)(2,1)}, u32[]{:S(2)}) %copy-start.1) | copy-done | bytes 1843224
  1.5 0.0 copy-start
  1.5 1.0 %shard_map.28 = bf16[16,464,128]{2,1,0:T(8,128)(2,1)S(1)} custom-call(bf16[4,240,960]{2,1,0:T(8,128)(2,1)S(1)} %copy-done.1), custom_call_target="tpu_custom_call" | custom-call | flops 20000000000 | bytes 40000000 | tf_op jit(solution)/shard_map/pallas_call | solution.py:169
  2.6 34.3 %all_to_all.10.b_ref = bf16[16,464,128]{2,1,0:T(8,128)(2,1)S(1)} all-to-all(bf16[16,464,128]{2,1,0:T(8,128)(2,1)S(1)} %shard_map.28), channel_id=1, replica_groups=mesh['vrow'=8,'aux'=8,'pair'=2] {'vrow','pair'}, dimensions={0} | all-to-all | bytes 3801088 | tf_op jit(solution)/shard_map/all_to_all | solution.py:177
  36.9 0.0 copy-done
  36.9 10.5 %shard_map.29 = f32[8,2,8,128]{3,2,1,0:T(8,128)S(1)} custom-call(bf16[16,464,128]{2,1,0:T(8,128)(2,1)S(1)} %all_to_all.10.b_ref, bf16[4,960,960]{2,1,0:T(8,128)(2,1)S(1)} %copy-done), custom_call_target="tpu_custom_call" | custom-call | tf_op jit(solution)/shard_map/pallas_call | solution.py:179
  47.3 0.1 collective-permute-start
  47.4 1.2 %collective-permute-done = f32[8,2,8,128]{3,2,1,0:T(8,128)S(1)} collective-permute-done((f32[8,2,8,128]{3,2,1,0:T(8,128)S(1)}, f32[8,2,8,128]{3,2,1,0:T(8,128)S(1)}, u32[]{:S(2)}, u32[]{:S(2)}) %collective-permute-start) | collective-permute-done | bytes 65568 | tf_op jit(solution)/shard_map/ppermute | solution.py:192
  48.7 17.5 %all_to_all.11 = f32[64,8,128]{2,1,0:T(8,128)S(1)} all-to-all(f32[64,8,128]{2,1,0:T(8,128)S(1)} %bitcast.3), channel_id=1, replica_groups={{0,1,4,5,8,9,12,13,16,17,20,21,24,25,28,29,32,33,36,37,40,41,44,45,48,4..., dimensions={0} | all-to-all | bytes 524288 | tf_op jit(solution)/shard_map/all_to_all | solution.py:195
  66.2 0.1 reduce_sum.9
  66.3 0.1 reshape.11
  66.4 0.6 copy.4
  (2 shorter events, 0.0 us)
Async XLA Ops:
  0.0 1.5 %copy-start.1 = (bf16[4,240,960]{2,1,0:T(8,128)(2,1)S(1)}, bf16[4,240,960]{2,1,0:T(8,128)(2,1)}, u32[]{:S(2)}) copy-start(bf16[4,240,960]{2,1,0:T(8,128)(2,1)} %f_ref.1) | copy-start | bytes 5529604
  1.5 35.3 %copy-start = (bf16[4,960,960]{2,1,0:T(8,128)(2,1)S(1)}, bf16[4,960,960]{2,1,0:T(8,128)(2,1)}, u32[]{:S(2)}) copy-start(bf16[4,960,960]{2,1,0:T(8,128)(2,1)} %t_ref.1) | copy-start | bytes 22118404
  47.3 1.3 %collective-permute-start = (f32[8,2,8,128]{3,2,1,0:T(8,128)S(1)}, f32[8,2,8,128]{3,2,1,0:T(8,128)S(1)}, u32[]{:S(2)}, u32[]{:S(2)}) collective-permute-start(f32[8,2,8,128]{3,2,1,0:T(8,128)S(1)} %shard_map.29), channel_id=1, source_target_pairs={{0,2},{2,0},{4,6},{6,4},{8,10},{10,8},{12,14},{14,12},{1,3},{3,1},... | collective-permute-start | bytes 196616 | tf_op jit(solution)/shard_map/ppermute | solution.py:192

commit v6 on v5

--- a/solution.py
+++ b/solution.py
@@ -30,19 +30,22 @@
 
 def pack_kernel(f_ref, out_ref):
     nq = f_ref.shape[1]
-    shape = (HEAD + 3 * 16, NA * 32)
-    row, col = iota(shape, 0), iota(shape, 1)
-    slot, a = row >> 2 & 3, row & 3
-    q = jnp.where(row < HEAD, row >> 2, FULL * G + jnp.where(slot == 3, (row - HEAD) >> 4, slot))
+    rows_of = HEAD + 16
+    row, col = iota((rows_of, NA * 32), 0), iota((rows_of, NA * 32), 1)
+    q, place = row >> 2, (row & 3) * 32
+    row, at = iota((3 * 16, NA * 32), 0), iota((3 * 16, NA * 32), 1)
+    slot, place4 = FULL * G + (row >> 4), (row & 3) * 32
+    fourth = (row & 15) >= 3 * NA
     spread = iota((16, 128), 0) >= 3 * NA
     for j in range(NB):
         base = min(NQ * j // 16 * 16, nq - 32)
-        pick = jnp.where(col == a * 32 + q + (NQ * j - base), 1.0, 0.0).astype(jnp.bfloat16)
+        offset = NQ * j - base
+        pick = jnp.where((col == place + q + offset) & (q < NQ), 1.0, 0.0).astype(jnp.bfloat16)
+        pick4 = jnp.where((at == place4 + slot + offset) & fourth, 1.0, 0.0).astype(jnp.bfloat16)
         window = f_ref[:, base : base + 32, :].reshape(NA * 32, V)
         rows = jnp.dot(pick, window, preferred_element_type=jnp.float32).astype(jnp.bfloat16)
-
-        def tile(start, k):
-            return rows[start : start + 16, k * 128 : (k + 1) * 128]
+        extra = window[:, SPREAD * 128 : (SPREAD + 1) * 128]
+        extra = jnp.dot(pick4, extra, preferred_element_type=jnp.float32).astype(jnp.bfloat16)
 
         for k in range(TILES):
             out_ref[j, k * HEAD : (k + 1) * HEAD, :] = rows[:HEAD, k * 128 : (k + 1) * 128]
@@ -50,9 +53,9 @@
             tails = [rows[32 * i : 32 * i + 16, MAIN:], rows[32 * i + 16 : 32 * i + 32, MAIN:]]
             out_ref[j, TAIL + 16 * i : TAIL + 16 * i + 16, :] = jnp.concatenate(tails, axis=1)
         for i, k in enumerate(LAST_TILES):
-            last = tile(HEAD, k)
+            last = rows[HEAD:, k * 128 : (k + 1) * 128]
             if i < 3:
-                last = jnp.where(spread, tile(HEAD + 16 * i, SPREAD), last)
+                last = jnp.where(spread, extra[16 * i : 16 * i + 16], last)
             out_ref[j, LAST + 16 * i : LAST + 16 * i + 16, :] = last
 
 
@@ -190,10 +193,11 @@
         compiler_params=pltpu.CompilerParams(vmem_limit_bytes=28 * MIB),
     )(mine, amplitudes)
     terms = terms + lax.ppermute(terms, "aux", [(i, i ^ 1) for i in range(8)])
+    terms = terms.astype(jnp.bfloat16)
     terms = jnp.broadcast_to(terms[:, None], (8, 4, 2, 8, 128)).reshape(64, 8, 128)
     groups = [[(v * 8 + 2 * x + c) * 2 + p for v in range(8) for x in range(4) for p in range(2)] for c in range(2)]
     terms = lax.all_to_all(terms, ALL, split_axis=0, concat_axis=0, tiled=True, axis_index_groups=groups)
-    total = jnp.sum(terms, axis=0).reshape(2, NA, npairs // 2, NB * NA)
+    total = jnp.sum(terms.astype(jnp.float32), axis=0).reshape(2, NA, npairs // 2, NB * NA)
     return jnp.transpose(total, (2, 0, 1, 3)).reshape(npairs, NA, NB * NA)
 
 

time: 67.2 us -> 66.1 us (0.984)
  blocking collectives: 51.8 us -> 50.9 us
    all_to_all x1, blocking collectives: 17.5 us -> 16.6 us  [local(): lax.all_to_all(terms, ALL, split_axis=0, concat_axis=0, tiled=True, axis_...]
where the time goes in v6:
time: 66.1 us; the launch traced here: 65.9 us
  blocking collectives  50.9 us (77%)
  Pallas kernels  11.4 us (17%)
  local copies, waits for them, and re-layouts  2.25 us (3%)
  waiting for transfers between devices  1.24 us (2%)
    all_to_all x1, blocking collectives, local(): mine = lax.all_to_all(packed, ROWS, split_axis=0, concat_axis=0, tiled=True)  34.3 us
    all_to_all x1, blocking collectives, local(): lax.all_to_all(terms, ALL, split_axis=0, concat_axis=0, tiled=True, axis_...  16.6 us
    pallas_call x1, Pallas kernels, local(): pl.pallas_call(ladder_kernel, in_specs=[vmem, vmem], out_specs=vmem, out_...  10.5 us
    unnamed x4, local copies, waits for them, and re-layouts  1.55 us
  transfers between devices with their start and end apart: 1, of which 1 were waited for; matrix products, arithmetic and copies ran while one was open for 0% of the time, Pallas kernels for 0%

profile of v6, /device:TPU:0, one launch (start us, length us, event | category | flops | bytes accessed | tf_op | source)
XLA Modules:
  0.0 65.9 jit_solution(14309412378832403273)
XLA Ops:
  0.0 0.0 copy-start.1
  0.0 1.5 %copy-done.1 = bf16[4,240,960]{2,1,0:T(8,128)(2,1)S(1)} copy-done((bf16[4,240,960]{2,1,0:T(8,128)(2,1)S(1)}, bf16[4,240,960]{2,1,0:T(8,128)(2,1)}, u32[]{:S(2)}) %copy-start.1) | copy-done | bytes 1843224
  1.5 0.0 copy-start
  1.5 0.9 %shard_map.28 = bf16[16,464,128]{2,1,0:T(8,128)(2,1)S(1)} custom-call(bf16[4,240,960]{2,1,0:T(8,128)(2,1)S(1)} %copy-done.1), custom_call_target="tpu_custom_call" | custom-call | flops 20000000000 | bytes 40000000 | tf_op jit(solution)/shard_map/pallas_call | solution.py:172
  2.4 34.3 %all_to_all.10.b_ref = bf16[16,464,128]{2,1,0:T(8,128)(2,1)S(1)} all-to-all(bf16[16,464,128]{2,1,0:T(8,128)(2,1)S(1)} %shard_map.28), channel_id=1, replica_groups=mesh['vrow'=8,'aux'=8,'pair'=2] {'vrow','pair'}, dimensions={0} | all-to-all | bytes 3801088 | tf_op jit(solution)/shard_map/all_to_all | solution.py:180
  36.7 0.0 copy-done
  36.7 10.5 %shard_map.29 = f32[8,2,8,128]{3,2,1,0:T(8,128)S(1)} custom-call(bf16[16,464,128]{2,1,0:T(8,128)(2,1)S(1)} %all_to_all.10.b_ref, bf16[4,960,960]{2,1,0:T(8,128)(2,1)S(1)} %copy-done), custom_call_target="tpu_custom_call" | custom-call | tf_op jit(solution)/shard_map/pallas_call | solution.py:182
  47.2 0.1 collective-permute-start
  47.3 1.2 %collective-permute-done = f32[8,2,8,128]{3,2,1,0:T(8,128)S(1)} collective-permute-done((f32[8,2,8,128]{3,2,1,0:T(8,128)S(1)}, f32[8,2,8,128]{3,2,1,0:T(8,128)S(1)}, u32[]{:S(2)}, u32[]{:S(2)}) %collective-permute-start) | collective-permute-done | bytes 65568 | tf_op jit(solution)/shard_map/ppermute | solution.py:195
  48.6 16.6 %all_to_all.11 = bf16[64,8,128]{2,1,0:T(8,128)(2,1)S(1)} all-to-all(bf16[64,8,128]{2,1,0:T(8,128)(2,1)S(1)} %bitcast.3), channel_id=1, replica_groups={{0,1,4,5,8,9,12,13,16,17,20,21,24,25,28,29,32,33,36,37,40,41,44,45,48,4..., dimensions={0} | all-to-all | bytes 262144 | tf_op jit(solution)/shard_map/all_to_all | solution.py:199
  65.2 0.1 convert_reduce_fusion
  65.2 0.1 reshape.11
  65.3 0.6 copy.4
  (2 shorter events, 0.0 us)
Async XLA Ops:
  0.0 1.5 %copy-start.1 = (bf16[4,240,960]{2,1,0:T(8,128)(2,1)S(1)}, bf16[4,240,960]{2,1,0:T(8,128)(2,1)}, u32[]{:S(2)}) copy-start(bf16[4,240,960]{2,1,0:T(8,128)(2,1)} %f_ref.1) | copy-start | bytes 5529604
  1.5 35.2 %copy-start = (bf16[4,960,960]{2,1,0:T(8,128)(2,1)S(1)}, bf16[4,960,960]{2,1,0:T(8,128)(2,1)}, u32[]{:S(2)}) copy-start(bf16[4,960,960]{2,1,0:T(8,128)(2,1)} %t_ref.1) | copy-start | bytes 22118404
  47.2 1.3 %collective-permute-start = (f32[8,2,8,128]{3,2,1,0:T(8,128)S(1)}, f32[8,2,8,128]{3,2,1,0:T(8,128)S(1)}, u32[]{:S(2)}, u32[]{:S(2)}) collective-permute-start(f32[8,2,8,128]{3,2,1,0:T(8,128)S(1)} %shard_map.29), channel_id=1, source_target_pairs={{0,2},{2,0},{4,6},{6,4},{8,10},{10,8},{12,14},{14,12},{1,3},{3,1},... | collective-permute-start | bytes 196616 | tf_op jit(solution)/shard_map/ppermute | solution.py:195

commit v7 on v6

--- a/solution.py
+++ b/solution.py
@@ -92,9 +92,9 @@
 
     def last_group():
         r, c = iota((nlast, size), 0), iota((nlast, size), 1)
-        put = jnp.where(c == (r >> 2 & 15) * 16 + (r >> 6) * 4 + (r & 3), 1.0, 0.0).astype(jnp.bfloat16)
+        put = jnp.where(c == (NB - 1 - (r >> 2 & 15)) * 16 + (r >> 6) * 4 + (r & 3), 1.0, 0.0).astype(jnp.bfloat16)
         r, c = iota((NB * NA, size), 0), iota((NB * NA, size), 1)
-        get = jnp.where(c == (r >> 2) * 16 + 12 + (r & 3), 1.0, 0.0).astype(jnp.bfloat16)
+        get = jnp.where(c == (NB - 1 - (r >> 2)) * 16 + 12 + (r & 3), 1.0, 0.0).astype(jnp.bfloat16)
 
         def move(matrix, x):
             return jnp.dot(matrix, x, preferred_element_type=jnp.float32).astype(jnp.bfloat16)
@@ -152,7 +152,7 @@
     first = iota((NB, 8, size), 1) < 4
     pairs = [jnp.where(first, sums[p], sums[p + 1]).reshape(NB * 8, size) for p in range(0, npairs, 2)]
     r, l = iota((2 * size, 128), 0), iota((2 * size, 128), 1)
-    pick = jnp.where(l == (r >> 8) * 64 + (r >> 4 & 15) * 4 + (r & 3), 1.0, 0.0).astype(jnp.bfloat16)
+    pick = jnp.where(l == (r >> 8) * 64 + (NB - 1 - (r >> 4 & 15)) * 4 + (r & 3), 1.0, 0.0).astype(jnp.bfloat16)
     total = jnp.zeros((NB * 8, 128), jnp.float32)
     for term in split(jnp.concatenate(pairs, axis=1), 3):
         total += jnp.dot(term, pick, preferred_element_type=jnp.float32)
@@ -162,8 +162,13 @@
         jnp.concatenate([last_ref[p], last_ref[p + 2]], axis=1).reshape(NB // 2, 8, 128) for p in range(2)
     ]
     first = iota((NB // 2, 8, 128), 1) < 4
-    out_ref[:, 0] = total[:, 0] + jnp.where(first, even, pltpu.roll(odd, 4, 1))
-    out_ref[:, 1] = total[:, 1] + jnp.where(first, pltpu.roll(even, 4, 1), odd)
+    even, odd = [
+        jnp.where(first, even, pltpu.roll(odd, 4, 1)),
+        jnp.where(first, pltpu.roll(even, 4, 1), odd),
+    ]
+    for m in range(NB // 2):
+        out_ref[m, 0] = total[m, 0] + odd[NB // 2 - 1 - m]
+        out_ref[m, 1] = total[m, 1] + even[NB // 2 - 1 - m]
 
 
 def local(factors, amplitudes):
@@ -177,7 +182,8 @@
         compiler_params=pltpu.CompilerParams(vmem_limit_bytes=10 * MIB),
         cost_estimate=pl.CostEstimate(flops=2 * 10**10, bytes_accessed=4 * 10**7, transcendentals=0),
     )(factors)
-    mine = lax.all_to_all(packed, ROWS, split_axis=0, concat_axis=0, tiled=True)
+    groups = [[(v * 8 + x) * 2 + p for v in range(8) for p in range(2)][::-1] for x in range(8)]
+    mine = lax.all_to_all(packed, ALL, split_axis=0, concat_axis=0, tiled=True, axis_index_groups=groups)
     size = NB * 16
     terms = pl.pallas_call(
         ladder_kernel,
@@ -195,7 +201,9 @@
     terms = terms + lax.ppermute(terms, "aux", [(i, i ^ 1) for i in range(8)])
     terms = terms.astype(jnp.bfloat16)
     terms = jnp.broadcast_to(terms[:, None], (8, 4, 2, 8, 128)).reshape(64, 8, 128)
-    groups = [[(v * 8 + 2 * x + c) * 2 + p for v in range(8) for x in range(4) for p in range(2)] for c in range(2)]
+    groups = [
+        [(v * 8 + 2 * x + c) * 2 + p for v in range(8) for x in range(4) for p in range(2)][::-1] for c in range(2)
+    ]
     terms = lax.all_to_all(terms, ALL, split_axis=0, concat_axis=0, tiled=True, axis_index_groups=groups)
     total = jnp.sum(terms.astype(jnp.float32), axis=0).reshape(2, NA, npairs // 2, NB * NA)
     return jnp.transpose(total, (2, 0, 1, 3)).reshape(npairs, NA, NB * NA)

time: 66.1 us -> 62.6 us (0.947)
  blocking collectives: 50.9 us -> 47.4 us
    all_to_all x1, blocking collectives: 34.3 us -> 32.4 us  [local(): lax.all_to_all(packed, ALL, split_axis=0, concat_axis=0, tiled=True, axis...]
    all_to_all x1, blocking collectives: 16.6 us -> 15 us  [local(): lax.all_to_all(terms, ALL, split_axis=0, concat_axis=0, tiled=True, axis_...]
where the time goes in v7:
time: 62.6 us; the launch traced here: 62.5 us
  blocking collectives  47.4 us (76%)
  Pallas kernels  11.4 us (18%)
  local copies, waits for them, and re-layouts  2.25 us (4%)
  waiting for transfers between devices  1.24 us (2%)
    all_to_all x1, blocking collectives, local(): lax.all_to_all(packed, ALL, split_axis=0, concat_axis=0, tiled=True, axis...  32.4 us
    all_to_all x1, blocking collectives, local(): lax.all_to_all(terms, ALL, split_axis=0, concat_axis=0, tiled=True, axis_...  15 us
    pallas_call x1, Pallas kernels, local(): pl.pallas_call(ladder_kernel, in_specs=[vmem, vmem], out_specs=vmem, out_...  10.5 us
    unnamed x4, local copies, waits for them, and re-layouts  1.55 us
  transfers between devices with their start and end apart: 1, of which 1 were waited for; matrix products, arithmetic and copies ran while one was open for 0% of the time, Pallas kernels for 0%

profile of v7, /device:TPU:0, one launch (start us, length us, event | category | flops | bytes accessed | tf_op | source)
XLA Modules:
  0.0 62.5 jit_solution(9992746193288448416)
XLA Ops:
  0.0 0.0 copy-start.1
  0.0 1.5 %copy-done.1 = bf16[4,240,960]{2,1,0:T(8,128)(2,1)S(1)} copy-done((bf16[4,240,960]{2,1,0:T(8,128)(2,1)S(1)}, bf16[4,240,960]{2,1,0:T(8,128)(2,1)}, u32[]{:S(2)}) %copy-start.1) | copy-done | bytes 1843224
  1.5 0.0 copy-start
  1.5 0.9 %shard_map.28 = bf16[16,464,128]{2,1,0:T(8,128)(2,1)S(1)} custom-call(bf16[4,240,960]{2,1,0:T(8,128)(2,1)S(1)} %copy-done.1), custom_call_target="tpu_custom_call" | custom-call | flops 20000000000 | bytes 40000000 | tf_op jit(solution)/shard_map/pallas_call | solution.py:177
  2.4 32.4 %all_to_all.10.b_ref = bf16[16,464,128]{2,1,0:T(8,128)(2,1)S(1)} all-to-all(bf16[16,464,128]{2,1,0:T(8,128)(2,1)S(1)} %shard_map.28), channel_id=1, replica_groups={{113,112,97,96,81,80,65,64,49,48,33,32,17,16,1,0},{115,114,99,98,83,82,..., dimensions={0} | all-to-all | bytes 3801088 | tf_op jit(solution)/shard_map/all_to_all | solution.py:186
  34.9 0.0 copy-done
  34.9 10.5 %shard_map.29 = f32[8,2,8,128]{3,2,1,0:T(8,128)S(1)} custom-call(bf16[16,464,128]{2,1,0:T(8,128)(2,1)S(1)} %all_to_all.10.b_ref, bf16[4,960,960]{2,1,0:T(8,128)(2,1)S(1)} %copy-done), custom_call_target="tpu_custom_call" | custom-call | tf_op jit(solution)/shard_map/pallas_call | solution.py:188
  45.4 0.1 collective-permute-start
  45.4 1.2 %collective-permute-done = f32[8,2,8,128]{3,2,1,0:T(8,128)S(1)} collective-permute-done((f32[8,2,8,128]{3,2,1,0:T(8,128)S(1)}, f32[8,2,8,128]{3,2,1,0:T(8,128)S(1)}, u32[]{:S(2)}, u32[]{:S(2)}) %collective-permute-start) | collective-permute-done | bytes 65568 | tf_op jit(solution)/shard_map/ppermute | solution.py:201
  46.7 15.0 %all_to_all.11 = bf16[64,8,128]{2,1,0:T(8,128)(2,1)S(1)} all-to-all(bf16[64,8,128]{2,1,0:T(8,128)(2,1)S(1)} %bitcast.3), channel_id=1, replica_groups={{125,124,121,120,117,116,113,112,109,108,105,104,101,100,97,96,93,92,89..., dimensions={0} | all-to-all | bytes 262144 | tf_op jit(solution)/shard_map/all_to_all | solution.py:207
  61.7 0.1 convert_reduce_fusion
  61.8 0.1 reshape.11
  61.9 0.6 copy.4
  (2 shorter events, 0.0 us)
Async XLA Ops:
  0.0 1.5 %copy-start.1 = (bf16[4,240,960]{2,1,0:T(8,128)(2,1)S(1)}, bf16[4,240,960]{2,1,0:T(8,128)(2,1)}, u32[]{:S(2)}) copy-start(bf16[4,240,960]{2,1,0:T(8,128)(2,1)} %f_ref.1) | copy-start | bytes 5529604
  1.5 33.3 %copy-start = (bf16[4,960,960]{2,1,0:T(8,128)(2,1)S(1)}, bf16[4,960,960]{2,1,0:T(8,128)(2,1)}, u32[]{:S(2)}) copy-start(bf16[4,960,960]{2,1,0:T(8,128)(2,1)} %t_ref.1) | copy-start | bytes 22118404
  45.4 1.3 %collective-permute-start = (f32[8,2,8,128]{3,2,1,0:T(8,128)S(1)}, f32[8,2,8,128]{3,2,1,0:T(8,128)S(1)}, u32[]{:S(2)}, u32[]{:S(2)}) collective-permute-start(f32[8,2,8,128]{3,2,1,0:T(8,128)S(1)} %shard_map.29), channel_id=1, source_target_pairs={{0,2},{2,0},{4,6},{6,4},{8,10},{10,8},{12,14},{14,12},{1,3},{3,1},... | collective-permute-start | bytes 196616 | tf_op jit(solution)/shard_map/ppermute | solution.py:201

commit v8 on v7

--- a/solution.py
+++ b/solution.py
@@ -11,6 +11,9 @@
 ALL = ("vrow", "aux", "pair")
 V = 960
 NB = 16
+VROWS = (2, 7, 6, 5, 4, 3, 1, 0)
+XS = (2, 3, 1, 0)
+PAIRS = (1, 0)
 NA = 4
 NQ = 15
 G = 4
@@ -166,9 +169,9 @@
         jnp.where(first, even, pltpu.roll(odd, 4, 1)),
         jnp.where(first, pltpu.roll(even, 4, 1), odd),
     ]
-    for m in range(NB // 2):
-        out_ref[m, 0] = total[m, 0] + odd[NB // 2 - 1 - m]
-        out_ref[m, 1] = total[m, 1] + even[NB // 2 - 1 - m]
+    for device in range(NB):
+        v, p, at = device // 2, device % 2, NB - 1 - device
+        out_ref[VROWS.index(v), PAIRS.index(p)] = total[at // 2, at % 2] + (odd if p else even)[v]
 
 
 def local(factors, amplitudes):
@@ -201,9 +204,7 @@
     terms = terms + lax.ppermute(terms, "aux", [(i, i ^ 1) for i in range(8)])
     terms = terms.astype(jnp.bfloat16)
     terms = jnp.broadcast_to(terms[:, None], (8, 4, 2, 8, 128)).reshape(64, 8, 128)
-    groups = [
-        [(v * 8 + 2 * x + c) * 2 + p for v in range(8) for x in range(4) for p in range(2)][::-1] for c in range(2)
-    ]
+    groups = [[(v * 8 + 2 * x + c) * 2 + p for v in VROWS for x in XS for p in PAIRS] for c in range(2)]
     terms = lax.all_to_all(terms, ALL, split_axis=0, concat_axis=0, tiled=True, axis_index_groups=groups)
     total = jnp.sum(terms.astype(jnp.float32), axis=0).reshape(2, NA, npairs // 2, NB * NA)
     return jnp.transpose(total, (2, 0, 1, 3)).reshape(npairs, NA, NB * NA)

time: 62.6 us -> 61.2 us (0.978)
  blocking collectives: 47.4 us -> 46 us
    all_to_all x1, blocking collectives: 15 us -> 13.6 us  [local(): lax.all_to_all(terms, ALL, split_axis=0, concat_axis=0, tiled=True, axis_...]
where the time goes in v8:
time: 61.2 us; the launch traced here: 61.1 us
  blocking collectives  46 us (75%)
  Pallas kernels  11.4 us (19%)
  local copies, waits for them, and re-layouts  2.25 us (4%)
  waiting for transfers between devices  1.24 us (2%)
    all_to_all x1, blocking collectives, local(): lax.all_to_all(packed, ALL, split_axis=0, concat_axis=0, tiled=True, axis...  32.4 us
    all_to_all x1, blocking collectives, local(): lax.all_to_all(terms, ALL, split_axis=0, concat_axis=0, tiled=True, axis_...  13.6 us
    pallas_call x1, Pallas kernels, local(): pl.pallas_call(ladder_kernel, in_specs=[vmem, vmem], out_specs=vmem, out_...  10.5 us
    unnamed x4, local copies, waits for them, and re-layouts  1.55 us
    ppermute x1, waiting for transfers between devices, local(): terms = terms + lax.ppermute(terms, 'aux', [(i, i ^ 1) for i in range(8)])  1.24 us
  transfers between devices with their start and end apart: 1, of which 1 were waited for; matrix products, arithmetic and copies ran while one was open for 0% of the time, Pallas kernels for 0%

profile of v8, /device:TPU:0, one launch (start us, length us, event | category | flops | bytes accessed | tf_op | source)
XLA Modules:
  0.0 61.1 jit_solution(16366267031105482220)
XLA Ops:
  0.0 0.0 copy-start.1
  0.0 1.5 %copy-done.1 = bf16[4,240,960]{2,1,0:T(8,128)(2,1)S(1)} copy-done((bf16[4,240,960]{2,1,0:T(8,128)(2,1)S(1)}, bf16[4,240,960]{2,1,0:T(8,128)(2,1)}, u32[]{:S(2)}) %copy-start.1) | copy-done | bytes 1843224
  1.5 0.0 copy-start
  1.5 0.9 %shard_map.28 = bf16[16,464,128]{2,1,0:T(8,128)(2,1)S(1)} custom-call(bf16[4,240,960]{2,1,0:T(8,128)(2,1)S(1)} %copy-done.1), custom_call_target="tpu_custom_call" | custom-call | flops 20000000000 | bytes 40000000 | tf_op jit(solution)/shard_map/pallas_call | solution.py:180
  2.4 32.4 %all_to_all.10.b_ref = bf16[16,464,128]{2,1,0:T(8,128)(2,1)S(1)} all-to-all(bf16[16,464,128]{2,1,0:T(8,128)(2,1)S(1)} %shard_map.28), channel_id=1, replica_groups={{113,112,97,96,81,80,65,64,49,48,33,32,17,16,1,0},{115,114,99,98,83,82,..., dimensions={0} | all-to-all | bytes 3801088 | tf_op jit(solution)/shard_map/all_to_all | solution.py:189
  34.9 0.0 copy-done
  34.9 10.5 %shard_map.29 = f32[8,2,8,128]{3,2,1,0:T(8,128)S(1)} custom-call(bf16[16,464,128]{2,1,0:T(8,128)(2,1)S(1)} %all_to_all.10.b_ref, bf16[4,960,960]{2,1,0:T(8,128)(2,1)S(1)} %copy-done), custom_call_target="tpu_custom_call" | custom-call | tf_op jit(solution)/shard_map/pallas_call | solution.py:191
  45.4 0.1 collective-permute-start
  45.4 1.2 %collective-permute-done = f32[8,2,8,128]{3,2,1,0:T(8,128)S(1)} collective-permute-done((f32[8,2,8,128]{3,2,1,0:T(8,128)S(1)}, f32[8,2,8,128]{3,2,1,0:T(8,128)S(1)}, u32[]{:S(2)}, u32[]{:S(2)}) %collective-permute-start) | collective-permute-done | bytes 65568 | tf_op jit(solution)/shard_map/ppermute | solution.py:204
  46.7 13.6 %all_to_all.11 = bf16[64,8,128]{2,1,0:T(8,128)(2,1)S(1)} all-to-all(bf16[64,8,128]{2,1,0:T(8,128)(2,1)S(1)} %bitcast.3), channel_id=1, replica_groups={{41,40,45,44,37,36,33,32,121,120,125,124,117,116,113,112,105,104,109,10..., dimensions={0} | all-to-all | bytes 262144 | tf_op jit(solution)/shard_map/all_to_all | solution.py:208
  60.3 0.1 convert_reduce_fusion
  60.4 0.1 reshape.11
  60.4 0.6 copy.4
  (2 shorter events, 0.0 us)
Async XLA Ops:
  0.0 1.5 %copy-start.1 = (bf16[4,240,960]{2,1,0:T(8,128)(2,1)S(1)}, bf16[4,240,960]{2,1,0:T(8,128)(2,1)}, u32[]{:S(2)}) copy-start(bf16[4,240,960]{2,1,0:T(8,128)(2,1)} %f_ref.1) | copy-start | bytes 5529604
  1.5 33.3 %copy-start = (bf16[4,960,960]{2,1,0:T(8,128)(2,1)S(1)}, bf16[4,960,960]{2,1,0:T(8,128)(2,1)}, u32[]{:S(2)}) copy-start(bf16[4,960,960]{2,1,0:T(8,128)(2,1)} %t_ref.1) | copy-start | bytes 22118404
  45.4 1.3 %collective-permute-start = (f32[8,2,8,128]{3,2,1,0:T(8,128)S(1)}, f32[8,2,8,128]{3,2,1,0:T(8,128)S(1)}, u32[]{:S(2)}, u32[]{:S(2)}) collective-permute-start(f32[8,2,8,128]{3,2,1,0:T(8,128)S(1)} %shard_map.29), channel_id=1, source_target_pairs={{0,2},{2,0},{4,6},{6,4},{8,10},{10,8},{12,14},{14,12},{1,3},{3,1},... | collective-permute-start | bytes 196616 | tf_op jit(solution)/shard_map/ppermute | solution.py:204

commit v9 on v8

--- a/solution.py
+++ b/solution.py
@@ -202,11 +202,10 @@
         compiler_params=pltpu.CompilerParams(vmem_limit_bytes=28 * MIB),
     )(mine, amplitudes)
     terms = terms + lax.ppermute(terms, "aux", [(i, i ^ 1) for i in range(8)])
-    terms = terms.astype(jnp.bfloat16)
     terms = jnp.broadcast_to(terms[:, None], (8, 4, 2, 8, 128)).reshape(64, 8, 128)
     groups = [[(v * 8 + 2 * x + c) * 2 + p for v in VROWS for x in XS for p in PAIRS] for c in range(2)]
     terms = lax.all_to_all(terms, ALL, split_axis=0, concat_axis=0, tiled=True, axis_index_groups=groups)
-    total = jnp.sum(terms.astype(jnp.float32), axis=0).reshape(2, NA, npairs // 2, NB * NA)
+    total = jnp.sum(terms, axis=0).reshape(2, NA, npairs // 2, NB * NA)
     return jnp.transpose(total, (2, 0, 1, 3)).reshape(npairs, NA, NB * NA)
 
 

time: 61.2 us -> 62.2 us (1.016)
  blocking collectives: 46 us -> 47 us
    all_to_all x1, blocking collectives: 13.6 us -> 14.6 us  [local(): lax.all_to_all(terms, ALL, split_axis=0, concat_axis=0, tiled=True, axis_...]
where the time goes in v9:
time: 62.2 us; the launch traced here: 62 us
  blocking collectives  47 us (76%)
  Pallas kernels  11.4 us (18%)
  local copies, waits for them, and re-layouts  2.25 us (4%)
  waiting for transfers between devices  1.24 us (2%)
    all_to_all x1, blocking collectives, local(): lax.all_to_all(packed, ALL, split_axis=0, concat_axis=0, tiled=True, axis...  32.4 us
    all_to_all x1, blocking collectives, local(): lax.all_to_all(terms, ALL, split_axis=0, concat_axis=0, tiled=True, axis_...  14.6 us
    pallas_call x1, Pallas kernels, local(): pl.pallas_call(ladder_kernel, in_specs=[vmem, vmem], out_specs=vmem, out_...  10.5 us
    unnamed x4, local copies, waits for them, and re-layouts  1.55 us
  transfers between devices with their start and end apart: 1, of which 1 were waited for; matrix products, arithmetic and copies ran while one was open for 0% of the time, Pallas kernels for 0%

profile of v9, /device:TPU:0, one launch (start us, length us, event | category | flops | bytes accessed | tf_op | source)
XLA Modules:
  0.0 62.0 jit_solution(1644887486599040042)
XLA Ops:
  0.0 0.0 copy-start.1
  0.0 1.5 %copy-done.1 = bf16[4,240,960]{2,1,0:T(8,128)(2,1)S(1)} copy-done((bf16[4,240,960]{2,1,0:T(8,128)(2,1)S(1)}, bf16[4,240,960]{2,1,0:T(8,128)(2,1)}, u32[]{:S(2)}) %copy-start.1) | copy-done | bytes 1843224
  1.5 0.0 copy-start
  1.5 0.9 %shard_map.28 = bf16[16,464,128]{2,1,0:T(8,128)(2,1)S(1)} custom-call(bf16[4,240,960]{2,1,0:T(8,128)(2,1)S(1)} %copy-done.1), custom_call_target="tpu_custom_call" | custom-call | flops 20000000000 | bytes 40000000 | tf_op jit(solution)/shard_map/pallas_call | solution.py:180
  2.4 32.4 %all_to_all.10.b_ref = bf16[16,464,128]{2,1,0:T(8,128)(2,1)S(1)} all-to-all(bf16[16,464,128]{2,1,0:T(8,128)(2,1)S(1)} %shard_map.28), channel_id=1, replica_groups={{113,112,97,96,81,80,65,64,49,48,33,32,17,16,1,0},{115,114,99,98,83,82,..., dimensions={0} | all-to-all | bytes 3801088 | tf_op jit(solution)/shard_map/all_to_all | solution.py:189
  34.9 0.0 copy-done
  34.9 10.5 %shard_map.29 = f32[8,2,8,128]{3,2,1,0:T(8,128)S(1)} custom-call(bf16[16,464,128]{2,1,0:T(8,128)(2,1)S(1)} %all_to_all.10.b_ref, bf16[4,960,960]{2,1,0:T(8,128)(2,1)S(1)} %copy-done), custom_call_target="tpu_custom_call" | custom-call | tf_op jit(solution)/shard_map/pallas_call | solution.py:191
  45.4 0.1 collective-permute-start
  45.4 1.2 %collective-permute-done = f32[8,2,8,128]{3,2,1,0:T(8,128)S(1)} collective-permute-done((f32[8,2,8,128]{3,2,1,0:T(8,128)S(1)}, f32[8,2,8,128]{3,2,1,0:T(8,128)S(1)}, u32[]{:S(2)}, u32[]{:S(2)}) %collective-permute-start) | collective-permute-done | bytes 65568 | tf_op jit(solution)/shard_map/ppermute | solution.py:204
  46.7 14.6 %all_to_all.11 = f32[64,8,128]{2,1,0:T(8,128)S(1)} all-to-all(f32[64,8,128]{2,1,0:T(8,128)S(1)} %bitcast.3), channel_id=1, replica_groups={{41,40,45,44,37,36,33,32,121,120,125,124,117,116,113,112,105,104,109,10..., dimensions={0} | all-to-all | bytes 524288 | tf_op jit(solution)/shard_map/all_to_all | solution.py:207
  61.3 0.1 reduce_sum.9
  61.4 0.1 reshape.11
  61.4 0.6 copy.4
  (2 shorter events, 0.0 us)
Async XLA Ops:
  0.0 1.5 %copy-start.1 = (bf16[4,240,960]{2,1,0:T(8,128)(2,1)S(1)}, bf16[4,240,960]{2,1,0:T(8,128)(2,1)}, u32[]{:S(2)}) copy-start(bf16[4,240,960]{2,1,0:T(8,128)(2,1)} %f_ref.1) | copy-start | bytes 5529604
  1.5 33.3 %copy-start = (bf16[4,960,960]{2,1,0:T(8,128)(2,1)S(1)}, bf16[4,960,960]{2,1,0:T(8,128)(2,1)}, u32[]{:S(2)}) copy-start(bf16[4,960,960]{2,1,0:T(8,128)(2,1)} %t_ref.1) | copy-start | bytes 22118404
  45.4 1.3 %collective-permute-start = (f32[8,2,8,128]{3,2,1,0:T(8,128)S(1)}, f32[8,2,8,128]{3,2,1,0:T(8,128)S(1)}, u32[]{:S(2)}, u32[]{:S(2)}) collective-permute-start(f32[8,2,8,128]{3,2,1,0:T(8,128)S(1)} %shard_map.29), channel_id=1, source_target_pairs={{0,2},{2,0},{4,6},{6,4},{8,10},{10,8},{12,14},{14,12},{1,3},{3,1},... | collective-permute-start | bytes 196616 | tf_op jit(solution)/shard_map/ppermute | solution.py:204

commit v10 on v8

--- a/solution.py
+++ b/solution.py
@@ -157,7 +157,7 @@
     r, l = iota((2 * size, 128), 0), iota((2 * size, 128), 1)
     pick = jnp.where(l == (r >> 8) * 64 + (NB - 1 - (r >> 4 & 15)) * 4 + (r & 3), 1.0, 0.0).astype(jnp.bfloat16)
     total = jnp.zeros((NB * 8, 128), jnp.float32)
-    for term in split(jnp.concatenate(pairs, axis=1), 3):
+    for term in split(jnp.concatenate(pairs, axis=1), 2):
         total += jnp.dot(term, pick, preferred_element_type=jnp.float32)
     total = total.reshape(NB // 2, 2, 8, 128)
 

time: 61.2 us -> 61.2 us (level)
  no operation moved by 1% of the time
where the time goes in v10:
time: 61.2 us; the launch traced here: 61 us
  blocking collectives  46 us (75%)
  Pallas kernels  11.3 us (18%)
  local copies, waits for them, and re-layouts  2.25 us (4%)
  waiting for transfers between devices  1.24 us (2%)
    all_to_all x1, blocking collectives, local(): lax.all_to_all(packed, ALL, split_axis=0, concat_axis=0, tiled=True, axis...  32.4 us
    all_to_all x1, blocking collectives, local(): lax.all_to_all(terms, ALL, split_axis=0, concat_axis=0, tiled=True, axis_...  13.6 us
    pallas_call x1, Pallas kernels, local(): pl.pallas_call(ladder_kernel, in_specs=[vmem, vmem], out_specs=vmem, out_...  10.4 us
    unnamed x4, local copies, waits for them, and re-layouts  1.55 us
    ppermute x1, waiting for transfers between devices, local(): terms = terms + lax.ppermute(terms, 'aux', [(i, i ^ 1) for i in range(8)])  1.24 us
  transfers between devices with their start and end apart: 1, of which 1 were waited for; matrix products, arithmetic and copies ran while one was open for 0% of the time, Pallas kernels for 0%

profile of v10, /device:TPU:0, one launch (start us, length us, event | category | flops | bytes accessed | tf_op | source)
XLA Modules:
  0.0 61.0 jit_solution(6723879945029499950)
XLA Ops:
  0.0 0.0 copy-start.1
  0.0 1.5 %copy-done.1 = bf16[4,240,960]{2,1,0:T(8,128)(2,1)S(1)} copy-done((bf16[4,240,960]{2,1,0:T(8,128)(2,1)S(1)}, bf16[4,240,960]{2,1,0:T(8,128)(2,1)}, u32[]{:S(2)}) %copy-start.1) | copy-done | bytes 1843224
  1.5 0.0 copy-start
  1.5 0.9 %shard_map.28 = bf16[16,464,128]{2,1,0:T(8,128)(2,1)S(1)} custom-call(bf16[4,240,960]{2,1,0:T(8,128)(2,1)S(1)} %copy-done.1), custom_call_target="tpu_custom_call" | custom-call | flops 20000000000 | bytes 40000000 | tf_op jit(solution)/shard_map/pallas_call | solution.py:180
  2.4 32.4 %all_to_all.10.b_ref = bf16[16,464,128]{2,1,0:T(8,128)(2,1)S(1)} all-to-all(bf16[16,464,128]{2,1,0:T(8,128)(2,1)S(1)} %shard_map.28), channel_id=1, replica_groups={{113,112,97,96,81,80,65,64,49,48,33,32,17,16,1,0},{115,114,99,98,83,82,..., dimensions={0} | all-to-all | bytes 3801088 | tf_op jit(solution)/shard_map/all_to_all | solution.py:189
  34.9 0.0 copy-done
  34.9 10.4 %shard_map.29 = f32[8,2,8,128]{3,2,1,0:T(8,128)S(1)} custom-call(bf16[16,464,128]{2,1,0:T(8,128)(2,1)S(1)} %all_to_all.10.b_ref, bf16[4,960,960]{2,1,0:T(8,128)(2,1)S(1)} %copy-done), custom_call_target="tpu_custom_call" | custom-call | tf_op jit(solution)/shard_map/pallas_call | solution.py:191
  45.3 0.1 collective-permute-start
  45.4 1.2 %collective-permute-done = f32[8,2,8,128]{3,2,1,0:T(8,128)S(1)} collective-permute-done((f32[8,2,8,128]{3,2,1,0:T(8,128)S(1)}, f32[8,2,8,128]{3,2,1,0:T(8,128)S(1)}, u32[]{:S(2)}, u32[]{:S(2)}) %collective-permute-start) | collective-permute-done | bytes 65568 | tf_op jit(solution)/shard_map/ppermute | solution.py:204
  46.7 13.6 %all_to_all.11 = bf16[64,8,128]{2,1,0:T(8,128)(2,1)S(1)} all-to-all(bf16[64,8,128]{2,1,0:T(8,128)(2,1)S(1)} %bitcast.3), channel_id=1, replica_groups={{41,40,45,44,37,36,33,32,121,120,125,124,117,116,113,112,105,104,109,10..., dimensions={0} | all-to-all | bytes 262144 | tf_op jit(solution)/shard_map/all_to_all | solution.py:208
  60.3 0.1 convert_reduce_fusion
  60.3 0.1 reshape.11
  60.4 0.6 copy.4
  (2 shorter events, 0.0 us)
Async XLA Ops:
  0.0 1.5 %copy-start.1 = (bf16[4,240,960]{2,1,0:T(8,128)(2,1)S(1)}, bf16[4,240,960]{2,1,0:T(8,128)(2,1)}, u32[]{:S(2)}) copy-start(bf16[4,240,960]{2,1,0:T(8,128)(2,1)} %f_ref.1) | copy-start | bytes 5529604
  1.5 33.3 %copy-start = (bf16[4,960,960]{2,1,0:T(8,128)(2,1)S(1)}, bf16[4,960,960]{2,1,0:T(8,128)(2,1)}, u32[]{:S(2)}) copy-start(bf16[4,960,960]{2,1,0:T(8,128)(2,1)} %t_ref.1) | copy-start | bytes 22118404
  45.3 1.3 %collective-permute-start = (f32[8,2,8,128]{3,2,1,0:T(8,128)S(1)}, f32[8,2,8,128]{3,2,1,0:T(8,128)S(1)}, u32[]{:S(2)}, u32[]{:S(2)}) collective-permute-start(f32[8,2,8,128]{3,2,1,0:T(8,128)S(1)} %shard_map.29), channel_id=1, source_target_pairs={{0,2},{2,0},{4,6},{6,4},{8,10},{10,8},{12,14},{14,12},{1,3},{3,1},... | collective-permute-start | bytes 196616 | tf_op jit(solution)/shard_map/ppermute | solution.py:204

commit v11 on v8

--- a/solution.py
+++ b/solution.py
@@ -11,8 +11,8 @@
 ALL = ("vrow", "aux", "pair")
 V = 960
 NB = 16
-VROWS = (2, 7, 6, 5, 4, 3, 1, 0)
-XS = (2, 3, 1, 0)
+VROWS = (2, 0, 1, 3, 4, 5, 6, 7)
+XS = (2, 0, 1, 3)
 PAIRS = (1, 0)
 NA = 4
 NQ = 15

time: 61.2 us -> 61.2 us (level)
  no operation moved by 1% of the time
where the time goes in v11:
time: 61.2 us; the launch traced here: 61.1 us
  blocking collectives  46 us (75%)
  Pallas kernels  11.4 us (19%)
  local copies, waits for them, and re-layouts  2.25 us (4%)
  waiting for transfers between devices  1.24 us (2%)
    all_to_all x1, blocking collectives, local(): lax.all_to_all(packed, ALL, split_axis=0, concat_axis=0, tiled=True, axis...  32.4 us
    all_to_all x1, blocking collectives, local(): lax.all_to_all(terms, ALL, split_axis=0, concat_axis=0, tiled=True, axis_...  13.6 us
    pallas_call x1, Pallas kernels, local(): pl.pallas_call(ladder_kernel, in_specs=[vmem, vmem], out_specs=vmem, out_...  10.5 us
    unnamed x4, local copies, waits for them, and re-layouts  1.55 us
    ppermute x1, waiting for transfers between devices, local(): terms = terms + lax.ppermute(terms, 'aux', [(i, i ^ 1) for i in range(8)])  1.24 us
  transfers between devices with their start and end apart: 1, of which 1 were waited for; matrix products, arithmetic and copies ran while one was open for 0% of the time, Pallas kernels for 0%

profile of v11, /device:TPU:0, one launch (start us, length us, event | category | flops | bytes accessed | tf_op | source)
XLA Modules:
  0.0 61.1 jit_solution(9744504090036870779)
XLA Ops:
  0.0 0.0 copy-start.1
  0.0 1.5 %copy-done.1 = bf16[4,240,960]{2,1,0:T(8,128)(2,1)S(1)} copy-done((bf16[4,240,960]{2,1,0:T(8,128)(2,1)S(1)}, bf16[4,240,960]{2,1,0:T(8,128)(2,1)}, u32[]{:S(2)}) %copy-start.1) | copy-done | bytes 1843224
  1.5 0.0 copy-start
  1.5 0.9 %shard_map.28 = bf16[16,464,128]{2,1,0:T(8,128)(2,1)S(1)} custom-call(bf16[4,240,960]{2,1,0:T(8,128)(2,1)S(1)} %copy-done.1), custom_call_target="tpu_custom_call" | custom-call | flops 20000000000 | bytes 40000000 | tf_op jit(solution)/shard_map/pallas_call | solution.py:180
  2.4 32.4 %all_to_all.10.b_ref = bf16[16,464,128]{2,1,0:T(8,128)(2,1)S(1)} all-to-all(bf16[16,464,128]{2,1,0:T(8,128)(2,1)S(1)} %shard_map.28), channel_id=1, replica_groups={{113,112,97,96,81,80,65,64,49,48,33,32,17,16,1,0},{115,114,99,98,83,82,..., dimensions={0} | all-to-all | bytes 3801088 | tf_op jit(solution)/shard_map/all_to_all | solution.py:189
  34.9 0.0 copy-done
  34.9 10.5 %shard_map.29 = f32[8,2,8,128]{3,2,1,0:T(8,128)S(1)} custom-call(bf16[16,464,128]{2,1,0:T(8,128)(2,1)S(1)} %all_to_all.10.b_ref, bf16[4,960,960]{2,1,0:T(8,128)(2,1)S(1)} %copy-done), custom_call_target="tpu_custom_call" | custom-call | tf_op jit(solution)/shard_map/pallas_call | solution.py:191
  45.4 0.1 collective-permute-start
  45.4 1.2 %collective-permute-done = f32[8,2,8,128]{3,2,1,0:T(8,128)S(1)} collective-permute-done((f32[8,2,8,128]{3,2,1,0:T(8,128)S(1)}, f32[8,2,8,128]{3,2,1,0:T(8,128)S(1)}, u32[]{:S(2)}, u32[]{:S(2)}) %collective-permute-start) | collective-permute-done | bytes 65568 | tf_op jit(solution)/shard_map/ppermute | solution.py:204
  46.7 13.6 %all_to_all.11 = bf16[64,8,128]{2,1,0:T(8,128)(2,1)S(1)} all-to-all(bf16[64,8,128]{2,1,0:T(8,128)(2,1)S(1)} %bitcast.3), channel_id=1, replica_groups={{41,40,33,32,37,36,45,44,9,8,1,0,5,4,13,12,25,24,17,16,21,20,29,28,57,5..., dimensions={0} | all-to-all | bytes 262144 | tf_op jit(solution)/shard_map/all_to_all | solution.py:208
  60.3 0.1 convert_reduce_fusion
  60.4 0.1 reshape.11
  60.5 0.6 copy.4
  (2 shorter events, 0.0 us)
Async XLA Ops:
  0.0 1.5 %copy-start.1 = (bf16[4,240,960]{2,1,0:T(8,128)(2,1)S(1)}, bf16[4,240,960]{2,1,0:T(8,128)(2,1)}, u32[]{:S(2)}) copy-start(bf16[4,240,960]{2,1,0:T(8,128)(2,1)} %f_ref.1) | copy-start | bytes 5529604
  1.5 33.3 %copy-start = (bf16[4,960,960]{2,1,0:T(8,128)(2,1)S(1)}, bf16[4,960,960]{2,1,0:T(8,128)(2,1)}, u32[]{:S(2)}) copy-start(bf16[4,960,960]{2,1,0:T(8,128)(2,1)} %t_ref.1) | copy-start | bytes 22118404
  45.4 1.3 %collective-permute-start = (f32[8,2,8,128]{3,2,1,0:T(8,128)S(1)}, f32[8,2,8,128]{3,2,1,0:T(8,128)S(1)}, u32[]{:S(2)}, u32[]{:S(2)}) collective-permute-start(f32[8,2,8,128]{3,2,1,0:T(8,128)S(1)} %shard_map.29), channel_id=1, source_target_pairs={{0,2},{2,0},{4,6},{6,4},{8,10},{10,8},{12,14},{14,12},{1,3},{3,1},... | collective-permute-start | bytes 196616 | tf_op jit(solution)/shard_map/ppermute | solution.py:204
